TPU v7x, 256 devices: a whole 4x4x8 slice. The times are simulated.
256 devices in a mesh: ctx: 64 (over y, z, core), batch: 4 (over x).
Axes of the slice: x: 4, y: 4, z: 8, core: 2. Of those that a mesh axis runs over, the one named last changes fastest.
Arguments:
- cache_keys: bfloat16 [131072, 4096], P('ctx', 'batch'), parts along dimension 1
- cache_values: bfloat16 [131072, 4096], P('ctx', 'batch'), parts along dimension 1, may hold values from -6 to 6
- sketch_matrix: bfloat16 [1024, 160], replicated, may hold values from -0.1875 to 0.1875
- queries: bfloat16 [2, 64, 4096], P(None, 'batch'), parts along dimension 1
- visible: int32 [2, 64], P(None, 'batch'), parts along dimension 1, may hold values from 65536 to 131072, as said below
Outputs:
- rank_keys: bfloat16 [131072, 640], P('ctx', 'batch'), parts along dimension 1
- attended: bfloat16 [2, 64, 4096], P(None, 'batch'), parts along dimension 1
There are 4 independent parts, one for each index of `batch`. A program takes and returns all parts, laid end to end along the dimension named above; an argument that names none is the same for every part. Nothing has to cross between parts.
Inputs may be any that keep to these rules, and one draw needn't show every extreme that they name: `visible`: row 0 sees all 131072 positions in every step.
All inputs are finite; a program needn't handle non-finite values.
Results may differ from a plain program's by a relative error of at most 0.03.
The roundings to bfloat16 on the way count: a program that leaves them out, or rounds other values in their place, can miss the bound.
Values may be sent and summed in bfloat16 or wider, within the bound.
No kernel may reach another device: no remote copies, remote signals or barrier semaphores. Data moves between devices by JAX's collectives and lax.ppermute only.
A program may use at most 128 MiB of HBM per device.

v0:
```python
import math

import jax
import jax.numpy as jnp
from jax import lax
from jax.sharding import PartitionSpec as P

HEADS = 32
KV_HEADS = 8
HEAD_DIM = 128
RANK = 160
ROWS = 16
STEPS = 2


def merged_2(part, axis, combine):
    gathered = jax.tree.map(lambda a: lax.all_gather(a, axis), part)

    def take(source):
        return jax.tree.map(lambda a: lax.dynamic_index_in_dim(a, source, 0, False), gathered)

    return lax.fori_loop(
        1, lax.axis_size(axis), lambda source, state: combine(state, take(source)), take(0)
    )


def orthonormal(power_rows, gram):
    lower = jnp.linalg.cholesky(gram)
    return lax.linalg.triangular_solve(
        lower, power_rows, left_side=False, lower=True, transpose_a=True
    ).astype(jnp.bfloat16)


def combine(first, second):
    top = jnp.maximum(first[0], second[0])
    first_factor = jnp.exp(first[0] - top)
    second_factor = jnp.exp(second[0] - top)
    merged_total = first_factor * first[1] + second_factor * second[1]
    merged_output = first_factor[..., None] * first[2] + second_factor[..., None] * second[2]
    return (top, merged_total, merged_output)


def shards(cache_keys, cache_values, sketch_matrix, queries, visible):
    shard_rows = cache_keys.shape[0]
    group_size = HEADS // KV_HEADS
    score_scale = 1.0 / math.sqrt(HEAD_DIM)
    sketch_rows = jnp.dot(cache_keys, sketch_matrix, preferred_element_type=jnp.float32).astype(
        jnp.bfloat16
    )
    local_power = jnp.dot(cache_keys.T, sketch_rows, preferred_element_type=jnp.float32)
    power = lax.psum(local_power, "ctx")
    gram = jnp.dot(
        power.T, power, precision=lax.Precision.HIGHEST, preferred_element_type=jnp.float32
    )
    basis = orthonormal(power, gram)
    rank_keys = jnp.dot(cache_keys, basis, preferred_element_type=jnp.float32).astype(jnp.bfloat16)
    basis_groups = basis.reshape(KV_HEADS, HEAD_DIM, RANK)
    query_groups = queries.reshape(STEPS, ROWS, KV_HEADS, group_size, HEAD_DIM)
    projected = jnp.einsum(
        "trgqd,gdk->trgqk", query_groups, basis_groups, preferred_element_type=jnp.float32
    )
    projected = projected.astype(jnp.bfloat16).reshape(STEPS, ROWS * HEADS, RANK)
    value_groups = cache_values.reshape(shard_rows, KV_HEADS, HEAD_DIM)
    positions = lax.axis_index("ctx") * shard_rows + jnp.arange(shard_rows, dtype=jnp.int32)
    results = []
    for decode_step in range(STEPS):
        scores_scores = (
            jnp.dot(projected[decode_step], rank_keys.T, preferred_element_type=jnp.float32)
            * score_scale
        )
        scores_scores = scores_scores.reshape(ROWS, HEADS, shard_rows)
        scores_masked = positions[None, :] < visible[decode_step][:, None]
        scores_scores = jnp.where(scores_masked[:, None, :], scores_scores, jnp.float32(-1e30))
        local_top = jnp.max(scores_scores, axis=2)
        expo = jnp.where(
            scores_masked[:, None, :],
            jnp.exp(scores_scores - local_top[..., None]),
            jnp.float32(0.0),
        )
        total = jnp.sum(expo, axis=2)
        weights = expo.astype(jnp.bfloat16).reshape(ROWS, KV_HEADS, group_size, shard_rows)
        outputs = jnp.einsum(
            "rgqs,sgd->rgqd", weights, value_groups, preferred_element_type=jnp.float32
        )
        total, outputs = (total, outputs.reshape(ROWS, HEADS, HEAD_DIM))
        merged = merged_2((local_top, total, outputs), "ctx", combine)
        results.append((merged[2] / merged[1][..., None]).astype(jnp.bfloat16))
    attended = jnp.stack(results)
    return (rank_keys, attended.reshape(STEPS, ROWS, HEADS * HEAD_DIM))


def solution(mesh):
    in_specs = (P("ctx", "batch"), P("ctx", "batch"), P(), P(None, "batch", None), P(None, "batch"))
    out_specs = (P("ctx", "batch"), P(None, "batch", None))
    return jax.shard_map(shards, mesh=mesh, in_specs=in_specs, out_specs=out_specs, check_vma=False)
```

profile of v0, /device:TPU:1, one launch (start us, length us, event | category | flops | bytes accessed | tf_op | source)
XLA Modules:
  0.0 661.7 jit_solution(5685086661791962601)
XLA Ops:
  8.1 6.5 convolution_bitcast_fusion
  15.0 5.2 copy.56
  20.3 179.3 %all-reduce.5.cloned.1.call-done = f32[1024,160]{0,1:T(8,128)} async-done(((f32[1024,160]{0,1:T(8,128)}), f32[1024,160]{0,1:T(8,128)}) %all-reduce.5.cloned.1.call-update) | async-done | bytes 655376 | tf_op jit(solution)/shard_map/psum | solution.py:51
  199.6 2.0 fusion.57
  201.8 11.7 %cholesky.51 = f32[128,128]{1,0:T(8,128)S(1)} custom-call(f32[128,128]{1,0:T(8,128)S(1)} %cholesky.124), custom_call_target="Cholesky" | custom-call | tf_op jit(solution)/shard_map/jit(cholesky)/cholesky | solution.py:28
  213.6 9.8 %custom-call.14 = f32[1,128,128]{1,2,0:T(8,128)S(1)} custom-call(f32[1,128,128]{2,1,0:T(8,128)S(1)} %get-tuple-element.419), custom_call_target="InvertDiagBlocksLowerTriangular" | custom-call | tf_op jit(solution)/shard_map/jit(cholesky)/cholesky | solution.py:28
  223.7 2.9 cholesky.110
  229.4 20.1 %custom-call.15 = f32[2,128,128]{1,2,0:T(8,128)S(1)} custom-call(f32[2,128,128]{2,1,0:T(8,128)S(1)} %pad_maximum_fusion.1), custom_call_target="InvertDiagBlocksLowerTriangular" | custom-call | tf_op jit(solution)/shard_map/triangular_solve | solution.py:29
  252.2 3.7 convolution_convert_fusion
  257.0 2.9 fusion.17
  259.9 5.2 reshape.146
  265.3 7.0 %fusion.18 = f32[8,16,4,128]{3,1,2,0:T(8,128)S(1)} fusion(bf16[2048,8,128,1]{2,1,0,3:T(8,128)(2,1)} %bitcast.134, f32[16,8,4,2048]{3,2,1,0:T(4,128)} %reshape.146, f32[16,8,4]{0,2,1:T(4,128)S(1)} %copy.45, pred[16,2048]{1,0:T(8,128)(4,1)S(1)} %get-tuple-element.423), kind=kOutput, calls=%fused_computation.34 | convolution fusion | flops 272629760 | bytes 8685568 | tf_op jit(solution)/shard_map/rgqs,sgd->rgqd/dot_general | solution.py:82
  273.7 2.8 fusion.16
  276.5 5.2 reshape.144
  281.9 7.2 %fusion.20 = f32[8,16,4,128]{3,1,2,0:T(8,128)S(1)} fusion(bf16[2048,8,128,1]{2,1,0,3:T(8,128)(2,1)} %bitcast.135, f32[16,8,4,2048]{3,2,1,0:T(4,128)} %reshape.144, f32[16,8,4]{0,2,1:T(4,128)S(1)} %copy.40, pred[16,2048]{1,0:T(8,128)(4,1)S(1)} %get-tuple-element.422), kind=kOutput, calls=%fused_computation.36 | convolution fusion | flops 272629760 | bytes 8685568 | tf_op jit(solution)/shard_map/rgqs,sgd->rgqd/dot_general | solution.py:82
  289.9 3.4 fusion.7
  293.4 3.3 fusion.6
  296.9 49.7 %all_gather.36 = f32[64,16,32]{2,1,0:T(8,128)S(1)} all-gather(f32[1,16,32]{2,1,0:T(8,128)S(1)} %all_gather.35), channel_id=1, replica_groups=mesh['ctx'=64,'batch'=4] {'ctx'}, dimensions={0}, use_global_device_ids=true | all-gather | bytes 133120 | tf_op jit(solution)/shard_map/all_gather | solution.py:17
  346.6 48.7 %all_gather.38 = f32[64,16,32]{2,1,0:T(8,128)S(1)} all-gather(f32[1,16,32]{2,1,0:T(8,128)S(1)} %all_gather.37), channel_id=1, replica_groups=mesh['ctx'=64,'batch'=4] {'ctx'}, dimensions={0}, use_global_device_ids=true | all-gather | bytes 133120 | tf_op jit(solution)/shard_map/all_gather | solution.py:17
  395.3 48.6 %all_gather.31 = f32[64,16,32]{2,1,0:T(8,128)S(1)} all-gather(f32[1,16,32]{2,1,0:T(8,128)S(1)} %all_gather.30), channel_id=1, replica_groups=mesh['ctx'=64,'batch'=4] {'ctx'}, dimensions={0}, use_global_device_ids=true | all-gather | bytes 133120 | tf_op jit(solution)/shard_map/all_gather | solution.py:17
  443.9 48.6 %all_gather.33 = f32[64,16,32]{2,1,0:T(8,128)S(1)} all-gather(f32[1,16,32]{2,1,0:T(8,128)S(1)} %all_gather.32), channel_id=1, replica_groups=mesh['ctx'=64,'batch'=4] {'ctx'}, dimensions={0}, use_global_device_ids=true | all-gather | bytes 133120 | tf_op jit(solution)/shard_map/all_gather | solution.py:17
  493.5 79.6 %while.41 = (s32[]{:T(128)}, f32[16,32]{1,0:T(8,128)S(1)}, f32[16,32]{1,0:T(8,128)S(1)}, f32[16,32,128]{2,1,0:T(8,128)S(1)}, f32[64,16,32]{2,1,0:T(8,128)S(1)}, ...) while((s32[]{:T(128)}, f32[16,32]{1,0:T(8,128)S(1)}, ...), condition=%wide.region_12.13_spmd, body=%wide.region_11.12_spmd.sunk | while | flops 199685 | bytes 807063 | solution.py:22
  494.8 1.2 fusion.79
  496.1 1.2 fusion.79
  501.1 1.2 fusion.79
  502.4 1.2 fusion.79
  506.2 1.2 fusion.79
  507.4 1.2 fusion.79
  508.7 1.2 fusion.79
  512.5 1.2 fusion.79
  513.8 1.2 fusion.79
  515.0 1.2 fusion.79
  518.8 1.2 fusion.79
  520.1 1.2 fusion.79
  525.1 1.2 fusion.79
  526.4 1.2 fusion.79
  530.2 1.2 fusion.79
  531.5 1.2 fusion.79
  532.7 1.2 fusion.79
  536.5 1.2 fusion.79
  537.8 1.2 fusion.79
  539.0 1.2 fusion.79
  542.8 1.2 fusion.79
  544.1 1.2 fusion.79
  549.1 1.2 fusion.79
  550.4 1.2 fusion.79
  554.2 1.2 fusion.79
  574.3 79.6 %while.40 = (s32[]{:T(128)}, f32[16,32]{1,0:T(8,128)S(1)}, f32[16,32]{1,0:T(8,128)S(1)}, f32[16,32,128]{2,1,0:T(8,128)S(1)}, f32[64,16,32]{2,1,0:T(8,128)S(1)}, ...) while((s32[]{:T(128)}, f32[16,32]{1,0:T(8,128)S(1)}, ...), condition=%wide.region_8.9_spmd, body=%wide.region_7.8_spmd.sunk | while | flops 199685 | bytes 807063 | solution.py:22
  (299 shorter events, 137.9 us)
Async XLA Ops:
  7.2 1.0 copy-start
  7.2 7.6 %copy-start.5 = (s32[2,16]{1,0:T(2,128)S(1)}, s32[2,16]{1,0:T(2,128)}, u32[]{:S(2)}) copy-start(s32[2,16]{1,0:T(2,128)} %param.13) | copy-start | bytes 388
  7.2 7.6 %copy-start.4 = (bf16[2,16,4096]{2,1,0:T(8,128)(2,1)S(1)}, bf16[2,16,4096]{2,1,0:T(8,128)(2,1)}, u32[]{:S(2)}) copy-start(bf16[2,16,4096]{2,1,0:T(8,128)(2,1)} %param.12) | copy-start | bytes 786436
  7.2 192.4 %all-reduce.5.cloned.1.call-start = ((), (), s32[]{:S(2)}) async-start(), calls=%async_computation | async-start | bytes 1310720 | tf_op jit(solution)/shard_map/psum | solution.py:51
  14.7 477.8 %all-gather.5.cloned.1.call-start = ((), (), s32[]{:S(2)}) async-start(), calls=%async_computation.2 | async-start | bytes 17039360 | tf_op jit(solution)/shard_map/all_gather | solution.py:17
  199.6 49.9 %copy-start.2 = (f32[1024,160]{0,1:T(8,128)S(1)}, f32[1024,160]{0,1:T(8,128)}, u32[]{:S(2)}) copy-start(f32[1024,160]{0,1:T(8,128)} %all-reduce.5.cloned.1.call-done) | copy-start | bytes 1966084
  256.0 17.7 %copy-start.3 = (bf16[160,2048]{1,0:T(8,128)(2,1)}, bf16[160,2048]{1,0:T(8,128)(2,1)S(1)}, u32[]{:S(2)}) copy-start(bf16[160,2048]{1,0:T(8,128)(2,1)S(1)} %convolution_convert_fusion) | copy-start | bytes 1966084
  273.1 300.2 %all-gather.3.cloned.1.call-start = ((), (), s32[]{:S(2)}) async-start(), calls=%async_computation.1 | async-start | bytes 17039360 | tf_op jit(solution)/shard_map/all_gather | solution.py:17
  573.1 81.8 %copy-start.1 = (bf16[1024,160]{0,1:T(8,128)(2,1)S(1)}, bf16[1024,160]{0,1:T(8,128)(2,1)}, u32[]{:S(2)}) copy-start(bf16[1024,160]{0,1:T(8,128)(2,1)} %param.11) | copy-start | bytes 983044
Sparse Core Ops, SparseCore 0:
  14.8 184.7 all-reduce.4
  273.2 100.2 all-gather.4
  376.7 97.4 all-gather.2
where the time goes:
time: 674 us; the launch traced here: 662 us
  other arithmetic  209 us (31%)
  blocking collectives  196 us (29%)
  waiting for transfers between devices  179 us (27%)
  matrix products  35.4 us (5%)
  local copies, waits for them, and re-layouts  22.2 us (3%)
  between operations  15.7 us (2%)
    all_gather x4, blocking collectives, merged_2(): gathered = jax.tree.map(lambda a: lax.all_gather(a, axis), part)  196 us
    psum x1, waiting for transfers between devices, shards(): power = lax.psum(local_power, 'ctx')  179 us
    add x126, other arithmetic, combine(): first_factor[..., None] * first[2] + second_factor[..., None] * second[2]  153 us
    another operation x7, other arithmetic, orthonormal(): lower = jnp.linalg.cholesky(gram)  25.8 us
    another operation x6, other arithmetic, orthonormal(): lax.linalg.triangular_solve(lower, power_rows, left_side=False, lower=Tru...  20.3 us
    dot_general x2, matrix products, shards(): jnp.einsum('rgqs,sgd->rgqd', weights, value_groups, preferred_element_typ...  14.1 us
  transfers between devices with their start and end apart: 3, of which 1 were waited for; matrix products, arithmetic and copies ran while one was open for 16% of the time, Pallas kernels for 0%

commit v1 on v0

v1 whole, which is shorter than its diff:
```python
import math

import jax
import jax.numpy as jnp
from jax import lax
from jax.experimental import pallas as pl
from jax.experimental.pallas import tpu as pltpu
from jax.sharding import PartitionSpec as P

HEADS = 32
KV_HEADS = 8
HEAD_DIM = 128
RANK = 160
ROWS = 16
STEPS = 2
WIDTH = KV_HEADS * HEAD_DIM
GROUP = HEADS // KV_HEADS
QUERIES = STEPS * ROWS
STACKED = GROUP * QUERIES
NY = 4
NZ = 8
NC = 2
HALF = KV_HEADS // NC
CHUNK = HALF * STACKED // (NY * NZ)
SPLIT = 3
EXTRA = 8
VMEM_BYTES = 50 * 1024 * 1024
HIGH = lax.Precision.HIGHEST
BLOCK = 32
PANEL = 8
LANES = 128
SPARE = RANK - LANES
LOG_SCALE = math.log2(math.e) / math.sqrt(HEAD_DIM)
HIDDEN = -1e30


def params():
    return pltpu.CompilerParams(vmem_limit_bytes=VMEM_BYTES)


def vmem():
    return pl.BlockSpec(memory_space=pltpu.VMEM)


def hbm():
    return pl.BlockSpec(memory_space=pltpu.HBM)


def smem():
    return pl.BlockSpec(memory_space=pltpu.SMEM)


def nn(a, b, precision=None):
    return jnp.dot(a, b, precision=precision, preferred_element_type=jnp.float32)


def nt(a, b, precision=None):
    return lax.dot_general(
        a, b, (((1,), (1,)), ((), ())), precision=precision, preferred_element_type=jnp.float32
    )


def tn(a, b, precision=None):
    return lax.dot_general(
        a, b, (((0,), (0,)), ((), ())), precision=precision, preferred_element_type=jnp.float32
    )


def index(y, z, c):
    return (y * NZ + z) * NC + c


CORES = [[index(y, z, c) for y in range(NY) for z in range(NZ)] for c in range(NC)]


def across(x):
    pairs = [(i, i ^ 1) for i in range(NY * NZ * NC)]
    return lax.ppermute(x, "ctx", pairs)


def scatter(x):
    return lax.all_to_all(x, "ctx", 0, 0, axis_index_groups=CORES)


def gather(x):
    return scatter(jnp.broadcast_to(x, (NY * NZ, *x.shape)))


def power_kernel(
    core_ref, keys_ref, sketch_hbm, keep_ref, send_ref, keys_buf, sketch_ref, total_ref, sems, *, pieces
):
    block = keys_buf.shape[0] // pieces
    copies = []
    for i in range(pieces):
        rows = pl.ds(i * block, block)
        copies.append(
            pltpu.make_async_copy(keys_ref.at[rows, :], keys_buf.at[rows, :], sems.at[i])
        )
    copies.append(pltpu.make_async_copy(sketch_hbm, sketch_ref, sems.at[pieces]))
    for copy in (copies[pieces], *copies[:pieces]):
        copy.start()
    copies[pieces].wait()
    total, rows = None, None
    for i in range(pieces + 1):
        before = rows
        if i < pieces:
            copies[i].wait()
            keys = keys_buf[i * block : (i + 1) * block, :]
            rows = nt(keys, sketch_ref[...]).astype(jnp.bfloat16)
        if i:
            part = tn(before, keys_buf[(i - 1) * block : i * block, :])
            total = part if total is None else total + part
    total_ref[...] = total
    for at in range(KV_HEADS):
        group = jnp.bitwise_xor(core_ref[0] * HALF, at)
        lane = pl.multiple_of(group * HEAD_DIM, HEAD_DIM)
        out_ref = keep_ref if at < HALF else send_ref
        lo = at % HALF * RANK
        out_ref[lo : lo + RANK, :] = total_ref[:, pl.ds(lane, HEAD_DIM)]


def local_power(core, keys, sketch):
    positions = keys.shape[0]
    pieces = 4
    half = jax.ShapeDtypeStruct((HALF * RANK, HEAD_DIM), jnp.float32)
    return pl.pallas_call(
        lambda *refs: power_kernel(*refs, pieces=pieces),
        in_specs=[smem(), hbm(), hbm()],
        out_specs=[vmem(), vmem()],
        out_shape=[half, half],
        scratch_shapes=[
            pltpu.VMEM((positions, WIDTH), jnp.bfloat16),
            pltpu.VMEM((RANK, WIDTH), jnp.bfloat16),
            pltpu.VMEM((RANK, WIDTH), jnp.float32),
            pltpu.SemaphoreType.DMA((pieces + 1,)),
        ],
        compiler_params=params(),
    )(core, keys, sketch)


def deep(left, right, axis):
    (a, b, c), (d, e, f) = split(left, 3), split(right, 3)
    return jnp.concatenate([a, a, b, b, a, c], axis), jnp.concatenate([d, e, d, e, f, d], 0)


def eliminate(tiles, start):
    below = lax.broadcasted_iota(jnp.int32, (BLOCK, LANES), 0)
    done = []
    for panel in range(0, BLOCK, PANEL):
        at = start + panel
        own = tiles[at // LANES]
        columns = [
            jnp.broadcast_to(own[:, (at + j) % LANES : (at + j) % LANES + 1], own.shape)
            for j in range(PANEL)
        ]
        for j in range(PANEL):
            ratio = columns[j] * (1.0 / columns[j][j : j + 1])
            ratio = jnp.where(below[: BLOCK - panel] > j, ratio, 0.0)
            for m in range(j + 1, PANEL):
                columns[m] = columns[m] - ratio * columns[m][j : j + 1]
            tiles = [tile - ratio * tile[j : j + 1] for tile in tiles]
        done.append([tile[:PANEL] for tile in tiles])
        tiles = [tile[PANEL:] for tile in tiles]
    return [jnp.concatenate(pieces, axis=0) for pieces in zip(*done)]


def factor_inverse(gram, work_ref):
    row = lax.broadcasted_iota(jnp.int32, (BLOCK, LANES), 0)
    lane = lax.broadcasted_iota(jnp.int32, (BLOCK, LANES), 1)
    wide = lax.broadcasted_iota(jnp.int32, (RANK, 2 * LANES), 1)
    work_ref[...] = jnp.zeros_like(work_ref)
    work_ref[:, :RANK] = gram
    for lo in range(0, RANK, BLOCK):
        hi = lo + BLOCK
        own, offset = lo // LANES, lo % LANES
        identity = jnp.where(lane == row + SPARE, 1.0, 0.0)
        tiles = [work_ref[lo:hi, :LANES], work_ref[lo:hi, LANES:] + identity]
        tiles = eliminate(tiles, lo)
        moved = pltpu.roll(tiles[1], (offset - SPARE) % LANES, 1)
        tiles[1] = jnp.where(lane < SPARE, tiles[1], 0.0)
        diagonal = jnp.sum(jnp.where(lane == row + offset, tiles[own], 0.0), axis=1, keepdims=True)
        root = lax.rsqrt(diagonal)
        root = root * (1.5 - 0.5 * (diagonal * root) * root)
        inside = (lane >= offset) & (lane < offset + BLOCK)
        tiles[own] = jnp.where(inside, moved, tiles[own])
        rows = jnp.concatenate(tiles, axis=1) * root
        work_ref[lo:hi, :] = rows
        if hi < RANK:
            left = wide[hi:]
            rest = jnp.where((left >= lo) & (left < hi), 0.0, work_ref[hi:, :])
            work_ref[hi:, :] = rest - tn(*deep(rows[:, hi:RANK], rows, 0))
    row = lax.broadcasted_iota(jnp.int32, (RANK, 2 * LANES), 0)
    return jnp.where(wide <= row, work_ref[...], 0.0)[:, :RANK]


def split(x, count):
    out = []
    for _ in range(count):
        out.append(x.astype(jnp.bfloat16))
        x = x - out[-1].astype(jnp.float32)
    return out


def find_basis(core_ref, near_ref, far_ref, basis_ref, power_ref, work_ref):
    for at in range(KV_HEADS):
        group = jnp.bitwise_xor(core_ref[0] * HALF, at)
        lanes = pl.ds(pl.multiple_of(group * HEAD_DIM, HEAD_DIM), HEAD_DIM)
        source = near_ref if at < HALF else far_ref
        lo = at % HALF * RANK
        power_ref[:, lanes] = source[lo : lo + RANK, :]
    high, middle, low = split(power_ref[...], 3)
    cross = nt(high, middle) + nt(high, low)
    gram = nt(high, high) + (nt(middle, middle) + (cross + cross.T))
    inverse = factor_inverse(gram, work_ref)
    first, second = split(inverse, 2), (high, middle)
    left = jnp.concatenate([first[0], first[0], first[1]], axis=1)
    right = jnp.concatenate([second[0], second[1], second[0]], axis=0)
    basis_ref[...] = nn(left, right).astype(jnp.bfloat16)


def attend_kernel(
    core_ref,
    near_ref,
    far_ref,
    keys_ref,
    values_ref,
    queries_ref,
    limit_ref,
    rank_ref,
    keep_ref,
    send_ref,
    basis_ref,
    power_ref,
    work_ref,
    keys_buf,
    values_buf,
    masked_ref,
    projected_ref,
    scores_ref,
    sems,
):
    copies = [
        pltpu.make_async_copy(keys_ref, keys_buf, sems.at[0]),
        pltpu.make_async_copy(values_ref, values_buf, sems.at[1]),
        pltpu.make_async_copy(masked_ref.at[pl.ds(0, RANK), :], rank_ref, sems.at[2]),
    ]
    for copy in copies[:2]:
        copy.start()
    positions = keys_buf.shape[0]
    column = lax.broadcasted_iota(jnp.int32, (QUERIES, positions), 1)
    masked_ref[RANK:, :] = jnp.where(column < limit_ref[...], 0.0, HIDDEN).astype(jnp.bfloat16)
    row = lax.broadcasted_iota(jnp.int32, (STACKED, QUERIES), 0)
    lane = lax.broadcasted_iota(jnp.int32, (STACKED, QUERIES), 1)
    own_mask = jnp.where(row % QUERIES == lane, 1.0, 0.0).astype(jnp.bfloat16)
    find_basis(core_ref, near_ref, far_ref, basis_ref, power_ref, work_ref)
    copies[0].wait()
    for lo in range(0, positions, positions // 4):
        hi = lo + positions // 4
        rank = nt(basis_ref[...], keys_buf[lo:hi, :])
        masked_ref[:RANK, lo:hi] = rank.astype(jnp.bfloat16)
    copies[2].start()
    lane = lax.broadcasted_iota(jnp.int32, (STACKED, HEAD_DIM), 1)
    for half, out_ref in enumerate((send_ref, keep_ref)):
        start = jnp.bitwise_xor(core_ref[0], 1 - half) * HALF
        for at in range(HALF):
            g = start + at
            stacked = []
            for q in range(GROUP):
                own = pl.ds(pl.multiple_of((g * GROUP + q) * HEAD_DIM, HEAD_DIM), HEAD_DIM)
                stacked.append(queries_ref[:, own])
            stacked = jnp.concatenate(stacked, axis=0)
            lanes = pl.ds(pl.multiple_of(g * HEAD_DIM, HEAD_DIM), HEAD_DIM)
            rows = slice(at * STACKED, (at + 1) * STACKED)
            projected = nt(stacked, basis_ref[:, lanes]).astype(jnp.bfloat16)
            projected_ref[half, rows, :RANK] = projected
            projected_ref[half, rows, RANK:] = own_mask
        for lo in range(0, positions, positions // 4):
            hi = lo + positions // 4
            scores_ref[half, :, lo:hi] = nn(projected_ref[half], masked_ref[:, lo:hi])
        if half == 0:
            copies[1].wait()
        extras = jnp.zeros((STACKED, HEAD_DIM), jnp.float32)
        for pair in range(0, HALF, 2):
            weights = []
            for at in (pair, pair + 1):
                scores = scores_ref[half, at * STACKED : (at + 1) * STACKED, :]
                top = jnp.max(scores, axis=1, keepdims=True)
                expo = jnp.exp2((scores - top) * LOG_SCALE)
                total = jnp.sum(expo, axis=1, keepdims=True)
                weights.append(expo.astype(jnp.bfloat16))
                extras = jnp.where(lane == 2 * at, top * LOG_SCALE, extras)
                extras = jnp.where(lane == 2 * at + 1, total, extras)
            lanes = pl.ds(pl.multiple_of((start + pair) * HEAD_DIM, 2 * HEAD_DIM), 2 * HEAD_DIM)
            both = nn(jnp.concatenate(weights, axis=0), values_buf[:, lanes])
            out_ref[pair, :STACKED, :] = both[:STACKED, :HEAD_DIM]
            out_ref[pair + 1, :STACKED, :] = both[STACKED:, HEAD_DIM:]
        extras = extras.T
        for at in range(HALF):
            row = extras[2 * at : 2 * at + 2]
            out_ref[at, STACKED:, :] = jnp.concatenate([row] * (EXTRA // 2), axis=0)
    copies[2].wait()


def attend(core, near, far, keys, values, queries, limit):
    positions = keys.shape[0]
    return pl.pallas_call(
        attend_kernel,
        out_shape=[
            jax.ShapeDtypeStruct((RANK, positions), jnp.bfloat16),
            *[jax.ShapeDtypeStruct((HALF, STACKED + EXTRA, HEAD_DIM), jnp.float32)] * 2,
        ],
        in_specs=[smem(), vmem(), vmem(), hbm(), hbm(), vmem(), vmem()],
        out_specs=[hbm(), vmem(), vmem()],
        scratch_shapes=[
            pltpu.VMEM((RANK, WIDTH), jnp.bfloat16),
            pltpu.VMEM((RANK, WIDTH), jnp.float32),
            pltpu.VMEM((RANK, 2 * LANES), jnp.float32),
            pltpu.VMEM((positions, WIDTH), jnp.bfloat16),
            pltpu.VMEM((positions, WIDTH), jnp.bfloat16),
            pltpu.VMEM((RANK + QUERIES, positions), jnp.bfloat16),
            pltpu.VMEM((NC, HALF * STACKED, RANK + QUERIES), jnp.bfloat16),
            pltpu.VMEM((NC, HALF * STACKED, positions), jnp.float32),
            pltpu.SemaphoreType.DMA((3,)),
        ],
        compiler_params=params(),
    )(core, near, far, keys, values, queries, limit)


def columns(rows):
    pad = jnp.zeros((HEAD_DIM - rows.shape[0], rows.shape[1]), jnp.float32)
    return jnp.concatenate([rows, pad], axis=0).T


def terms(x):
    return [term.astype(jnp.float32) for term in split(x, SPLIT)]


def pair_kernel(keep_ref, sent_ref, out_ref):
    chunks = STACKED // CHUNK
    rest = jnp.zeros((EXTRA - 2 * SPLIT, STACKED), jnp.float32)
    factors, extras = [], []
    for g in range(HALF):
        tops = [ref[g, STACKED : STACKED + 1, :] for ref in (keep_ref, sent_ref)]
        totals = [ref[g, STACKED + 1 : STACKED + 2, :] for ref in (keep_ref, sent_ref)]
        top = jnp.maximum(*tops)
        pair = [jnp.exp2(t - top) for t in tops]
        total = pair[0] * totals[0] + pair[1] * totals[1]
        extras.append(jnp.concatenate([*terms(top), *terms(total), rest], axis=0))
        factors += pair
    factors = columns(jnp.concatenate(factors, axis=0))
    for g in range(HALF):
        numerator = factors[:, 2 * g : 2 * g + 1] * keep_ref[g, :STACKED]
        numerator += factors[:, 2 * g + 1 : 2 * g + 2] * sent_ref[g, :STACKED]
        for i in range(chunks):
            rows = numerator[i * CHUNK : (i + 1) * CHUNK]
            part = jnp.concatenate([rows, extras[g]], axis=0)
            out_ref[g * chunks + i] = part.astype(jnp.bfloat16)


def merge_pair(keep, sent):
    return pl.pallas_call(
        pair_kernel,
        out_shape=jax.ShapeDtypeStruct((NY * NZ, CHUNK + EXTRA, HEAD_DIM), jnp.bfloat16),
        in_specs=[vmem(), vmem()],
        out_specs=vmem(),
        compiler_params=params(),
    )(keep, sent)


def merge_kernel(at_ref, parts_ref, out_ref, factor_ref):
    count = parts_ref.shape[0]
    parts = parts_ref[...].astype(jnp.float32)
    extra = parts[:, CHUNK:, :]
    tops = sum(extra[:, i, :] for i in range(SPLIT))
    totals = sum(extra[:, SPLIT + i, :] for i in range(SPLIT))
    factors = jnp.exp2(tops - jnp.max(tops, axis=0, keepdims=True))
    total = jnp.sum(factors * totals, axis=0, keepdims=True)
    factor_ref[...] = columns(factors / total)
    own = factor_ref[pl.ds(pl.multiple_of(at_ref[0] * CHUNK, CHUNK), CHUNK), :]
    out = jnp.zeros((CHUNK, HEAD_DIM), jnp.float32)
    for i in range(count):
        out += own[:, i : i + 1] * parts[i, :CHUNK, :]
    out_ref[...] = out.astype(jnp.bfloat16)


def merge(at, parts):
    return pl.pallas_call(
        merge_kernel,
        out_shape=jax.ShapeDtypeStruct((CHUNK, HEAD_DIM), jnp.bfloat16),
        in_specs=[smem(), vmem()],
        out_specs=vmem(),
        scratch_shapes=[pltpu.VMEM((STACKED, HEAD_DIM), jnp.float32)],
        compiler_params=params(),
    )(at, parts)


def place_kernel(core_ref, near_ref, far_ref, out_ref):
    per_head = QUERIES // CHUNK
    for at in range(HEADS):
        head = jnp.bitwise_xor(core_ref[0] * (HEADS // NC), at)
        lanes = pl.ds(pl.multiple_of(head * HEAD_DIM, HEAD_DIM), HEAD_DIM)
        source = near_ref if at < HEADS // NC else far_ref
        lo = at % (HEADS // NC) * per_head
        for i in range(per_head):
            out_ref[i * CHUNK : (i + 1) * CHUNK, lanes] = source[lo + i]


def place(core, near, far):
    return pl.pallas_call(
        place_kernel,
        out_shape=jax.ShapeDtypeStruct((QUERIES, HEADS * HEAD_DIM), jnp.bfloat16),
        in_specs=[smem(), vmem(), vmem()],
        out_specs=vmem(),
        compiler_params=params(),
    )(core, near, far)


def summed(keep, send):
    part = (keep + across(send)).reshape(NY * NZ, -1, 4, HEAD_DIM)
    near = gather(jnp.sum(scatter(part), axis=0)).reshape(HALF * RANK, HEAD_DIM)
    return near, across(near)


def shards(cache_keys, cache_values, sketch_matrix, queries, visible):
    shard_rows = cache_keys.shape[0]
    me = lax.axis_index("ctx").astype(jnp.int32)
    core = (me % NC).reshape(1)
    near, far = summed(*local_power(core, cache_keys, pltpu.with_memory_space_constraint(sketch_matrix.T, pltpu.HBM)))
    limit = visible.reshape(QUERIES, 1) - me * shard_rows
    rank_keys, keep, send = attend(
        core, near, far, cache_keys, cache_values, queries.reshape(QUERIES, -1), limit
    )
    parts = scatter(merge_pair(keep, across(send)))
    chunk = merge((me // NC % (STACKED // CHUNK)).reshape(1), parts)
    near = gather(chunk)
    attended = place(core, near, across(near))
    return rank_keys.T, attended.reshape(STEPS, ROWS, HEADS * HEAD_DIM)


def solution(mesh):
    in_specs = (P("ctx", "batch"), P("ctx", "batch"), P(), P(None, "batch", None), P(None, "batch"))
    out_specs = (P("ctx", "batch"), P(None, "batch", None))
    return jax.shard_map(shards, mesh=mesh, in_specs=in_specs, out_specs=out_specs, check_vma=False)
```

time: 674 us -> 103 us (0.15); the launches traced: 662 us -> 102 us
  other arithmetic: 209 us -> 0.11 us
  waiting for transfers between devices: 179 us -> 14 us
  blocking collectives: 196 us -> 51.4 us
  matrix products: 35.4 us -> 0 us
  local copies, waits for them, and re-layouts: 22.2 us -> 0.16 us
  Pallas kernels: 0 us -> 20.2 us
  starting transfers between devices: 0.29 us -> 15.6 us
  between operations: 15.7 us -> 0.74 us
    all_gather x4 -> x0, blocking collectives: 196 us -> none  [merged_2(): gathered = jax.tree.map(lambda a: lax.all_gather(a, axis), part)]
    psum x1 -> x0, waiting for transfers between devices: 179 us -> none  [shards(): power = lax.psum(local_power, 'ctx')]
    add x253 -> x1, other arithmetic: 155 us -> 0.03 us  [summed(): part = (keep + across(send)).reshape(NY * NZ, -1, 4, HEAD_DIM)]
    all_to_all x0 -> x3, blocking collectives: none -> 51.4 us  [scatter(): return lax.all_to_all(x, 'ctx', 0, 0, axis_index_groups=CORES)]
    another operation x14 -> x0, other arithmetic: 46.8 us -> none  [the longest x7 25.8 us: orthonormal(): lower = jnp.linalg.cholesky(gram)]
    dot_general x8 -> x0, matrix products: 32.5 us -> none  [the longest x2 14.1 us: shards(): jnp.einsum('rgqs,sgd->rgqd', weights, value_groups, preferred_element_typ...]
    pallas_call x0 -> x5, Pallas kernels: none -> 20.2 us  [the longest x1 13.3 us: attend(): pl.pallas_call(attend_kernel, out_shape=[jax.ShapeDtypeStruct((RANK, posi...]
    ppermute x0 -> x4, starting transfers between devices: none -> 11.1 us  [across(): return lax.ppermute(x, 'ctx', pairs)]
  transfers between devices with their start and end apart: 3 -> 5, of which waited for: 1 -> 5; matrix products, arithmetic and copies ran while one was open for 16% -> 0% of each run, Pallas kernels for 0% -> 0%
where the time goes in v1:
time: 103 us; the launch traced here: 102 us
  blocking collectives  51.4 us (50%)
  Pallas kernels  20.2 us (20%)
  starting transfers between devices  15.6 us (15%)
  waiting for transfers between devices  14 us (14%)
    all_to_all x3, blocking collectives, scatter(): return lax.all_to_all(x, 'ctx', 0, 0, axis_index_groups=CORES)  51.4 us
    pallas_call x1, Pallas kernels, attend(): pl.pallas_call(attend_kernel, out_shape=[jax.ShapeDtypeStruct((RANK, posi...  13.3 us
    ppermute x4, starting transfers between devices, across(): return lax.ppermute(x, 'ctx', pairs)  11.1 us
    all_to_all x1, waiting for transfers between devices, scatter(): return lax.all_to_all(x, 'ctx', 0, 0, axis_index_groups=CORES)  9.36 us
    pallas_call x1, Pallas kernels, local_power(): pl.pallas_call(lambda *refs: power_kernel(*refs, pieces=pieces), in_specs...  4.75 us
    ppermute x4, waiting for transfers between devices, across(): return lax.ppermute(x, 'ctx', pairs)  4.59 us
    all_to_all x1, starting transfers between devices, scatter(): return lax.all_to_all(x, 'ctx', 0, 0, axis_index_groups=CORES)  4.5 us
  transfers between devices with their start and end apart: 5, of which 5 were waited for; matrix products, arithmetic and copies ran while one was open for 0% of the time, Pallas kernels for 0%

profile of v1, /device:TPU:1, one launch (start us, length us, event | category | flops | bytes accessed | tf_op | source)
XLA Modules:
  0.0 102.2 jit_solution(2359624395666854555)
XLA Ops:
  0.6 0.0 copy-start.1
  0.6 0.0 copy-start
  0.7 4.8 %shard_map.68 = (f32[640,128]{1,0:T(8,128)S(1)}, f32[640,128]{1,0:T(8,128)S(1)}) custom-call(s32[1]{0:T(128)} %bitcast.refs_0_.core_ref, bf16[2048,1024]{1,0:T(8,128)(2,1)} %keys_ref.1, bf16[160,1024]{1,0:T(8,128)(2,1)} %bitcast.12), custom_call_target="tpu_custom_call" | custom-call | tf_op jit(solution)/shard_map/pallas_call | solution.py:126
  5.4 3.3 %collective-permute-start = (f32[640,128]{1,0:T(8,128)S(1)}, f32[640,128]{1,0:T(8,128)S(1)}, u32[]{:S(2)}, u32[]{:S(2)}) collective-permute-start(f32[640,128]{1,0:T(8,128)S(1)} %get-tuple-element.8), channel_id=1, source_target_pairs={{0,4},{4,0},{8,12},{12,8},{16,20},{20,16},{24,28},{28,24},{32,36},... | collective-permute-start | bytes 983048 | tf_op jit(solution)/shard_map/ppermute | solution.py:78
  8.8 1.3 %collective-permute-done = f32[640,128]{1,0:T(8,128)S(1)} collective-permute-done((f32[640,128]{1,0:T(8,128)S(1)}, f32[640,128]{1,0:T(8,128)S(1)}, u32[]{:S(2)}, u32[]{:S(2)}) %collective-permute-start) | collective-permute-done | bytes 327712 | tf_op jit(solution)/shard_map/ppermute | solution.py:78
  10.0 19.7 %all_to_all.20 = f32[32,5,4,128]{3,2,1,0:T(4,128)S(1)} all-to-all(f32[32,5,4,128]{3,2,1,0:T(4,128)S(1)} %bitcast.11), channel_id=1, replica_groups={{0,8,16,24,32,40,48,56,64,72,80,88,96,104,112,120,128,136,144,152,160,1..., dimensions={0} | all-to-all | bytes 655360 | tf_op jit(solution)/shard_map/all_to_all | solution.py:82
  29.8 0.1 reduce_sum.9
  29.9 17.3 %all_to_all.21 = f32[32,5,4,128]{3,2,1,0:T(4,128)S(1)} all-to-all(f32[32,5,4,128]{3,2,1,0:T(4,128)S(1)} %broadcast_in_dim.6), channel_id=1, replica_groups={{0,8,16,24,32,40,48,56,64,72,80,88,96,104,112,120,128,136,144,152,160,1..., dimensions={0} | all-to-all | bytes 655360 | tf_op jit(solution)/shard_map/all_to_all | solution.py:82
  47.2 4.5 %collective-permute-start.1 = (f32[640,128]{1,0:T(8,128)S(1)}, f32[640,128]{1,0:T(8,128)S(1)}, u32[]{:S(2)}, u32[]{:S(2)}) collective-permute-start(f32[640,128]{1,0:T(8,128)S(1)} %bitcast.8), channel_id=1, source_target_pairs={{0,4},{4,0},{8,12},{12,8},{16,20},{20,16},{24,28},{28,24},{32,36},... | collective-permute-start | bytes 983048 | tf_op jit(solution)/shard_map/ppermute | solution.py:78
  51.6 0.0 copy-done.1
  51.6 0.1 sub.16.limit_ref
  51.7 1.2 %collective-permute-done.1.far_ref = f32[640,128]{1,0:T(8,128)S(1)} collective-permute-done((f32[640,128]{1,0:T(8,128)S(1)}, f32[640,128]{1,0:T(8,128)S(1)}, u32[]{:S(2)}, u32[]{:S(2)}) %collective-permute-start.1) | collective-permute-done | bytes 327712 | tf_op jit(solution)/shard_map/ppermute | solution.py:78
  52.9 0.0 copy-done
  52.9 13.3 %shard_map.69 = (bf16[160,2048]{1,0:T(8,128)(2,1)}, f32[4,136,128]{2,1,0:T(8,128)S(1)}, f32[4,136,128]{2,1,0:T(8,128)S(1)}) custom-call(s32[1]{0:T(128)} %bitcast.refs_0_.core_ref, f32[640,128]{1,0:T(8,128)S(1)} %bitcast.9, f32[640,128]{1,0:T(8,128)S(1)} %collective-permute-done.1.far_ref, bf16[2048,1024]{1,0:T(8,128)(2,1)} %keys_ref.1, ...), custom_call_target="tpu_custom_call" | custom-call | tf_op jit(solution)/shard_map/pallas_call | solution.py:306
  66.2 0.5 collective-permute-start.2
  66.7 1.2 %collective-permute-done.2.sent_ref = f32[4,136,128]{2,1,0:T(8,128)S(1)} collective-permute-done((f32[4,136,128]{2,1,0:T(8,128)S(1)}, f32[4,136,128]{2,1,0:T(8,128)S(1)}, u32[]{:S(2)}, u32[]{:S(2)}) %collective-permute-start.2) | collective-permute-done | bytes 278560 | tf_op jit(solution)/shard_map/ppermute | solution.py:78
  67.9 1.0 %shard_map.70 = bf16[32,24,128]{2,1,0:T(8,128)(2,1)} custom-call(f32[4,136,128]{2,1,0:T(8,128)S(1)} %get-tuple-element.10.keep_ref, f32[4,136,128]{2,1,0:T(8,128)S(1)} %collective-permute-done.2.sent_ref), custom_call_target="tpu_custom_call" | custom-call | tf_op jit(solution)/shard_map/pallas_call | solution.py:361
  68.9 4.5 %all-to-all-start.2 = ((bf16[32,24,128]{2,1,0:T(8,128)(2,1)}), bf16[32,24,128]{2,1,0:T(8,128)(2,1)S(1)}, u32[]{:S(2)}, u32[]{:S(2)}) async-start(bf16[32,24,128]{2,1,0:T(8,128)(2,1)} %shard_map.70), calls=%async_computation.2 | async-start | bytes 393216 | tf_op jit(solution)/shard_map/all_to_all | solution.py:82
  73.5 9.4 %all-to-all-done.2.parts_ref = bf16[32,24,128]{2,1,0:T(8,128)(2,1)S(1)} async-done(((bf16[32,24,128]{2,1,0:T(8,128)(2,1)}), bf16[32,24,128]{2,1,0:T(8,128)(2,1)S(1)}, u32[]{:S(2)}, u32[]{:S(2)}) %all-to-all-start.2) | async-done | bytes 196640 | tf_op jit(solution)/shard_map/all_to_all | solution.py:82
  82.8 0.4 shard_map.71
  83.2 14.4 %all_to_all.22.near_ref = bf16[32,16,128]{2,1,0:T(8,128)(2,1)S(1)} all-to-all(bf16[32,16,128]{2,1,0:T(8,128)(2,1)S(1)} %broadcast_in_dim.7), channel_id=1, replica_groups={{0,8,16,24,32,40,48,56,64,72,80,88,96,104,112,120,128,136,144,152,160,1..., dimensions={0} | all-to-all | bytes 262144 | tf_op jit(solution)/shard_map/all_to_all | solution.py:82
  97.6 2.9 %collective-permute-start.3 = (bf16[32,16,128]{2,1,0:T(8,128)(2,1)S(1)}, bf16[32,16,128]{2,1,0:T(8,128)(2,1)S(1)}, u32[]{:S(2)}, u32[]{:S(2)}) collective-permute-start(bf16[32,16,128]{2,1,0:T(8,128)(2,1)S(1)} %all_to_all.22.near_ref), channel_id=1, source_target_pairs={{0,4},{4,0},{8,12},{12,8},{16,20},{20,16},{24,28},{28,24},{32,36},... | collective-permute-start | bytes 393224 | tf_op jit(solution)/shard_map/ppermute | solution.py:78
  100.5 1.0 collective-permute-done.3.far_ref
  101.5 0.8 shard_map.72
  (4 shorter events, 0.1 us)
Async XLA Ops:
  0.6 51.0 %copy-start.1 = (s32[2,16]{1,0:T(2,128)S(1)}, s32[2,16]{1,0:T(2,128)}, u32[]{:S(2)}) copy-start(s32[2,16]{1,0:T(2,128)} %param.9) | copy-start | bytes 388
  0.6 52.3 %copy-start = (bf16[2,16,4096]{2,1,0:T(8,128)(2,1)S(1)}, bf16[2,16,4096]{2,1,0:T(8,128)(2,1)}, u32[]{:S(2)}) copy-start(bf16[2,16,4096]{2,1,0:T(8,128)(2,1)} %param.8) | copy-start | bytes 786436
  5.4 4.6 %collective-permute-start = (f32[640,128]{1,0:T(8,128)S(1)}, f32[640,128]{1,0:T(8,128)S(1)}, u32[]{:S(2)}, u32[]{:S(2)}) collective-permute-start(f32[640,128]{1,0:T(8,128)S(1)} %get-tuple-element.8), channel_id=1, source_target_pairs={{0,4},{4,0},{8,12},{12,8},{16,20},{20,16},{24,28},{28,24},{32,36},... | collective-permute-start | bytes 983048 | tf_op jit(solution)/shard_map/ppermute | solution.py:78
  47.2 5.7 %collective-permute-start.1 = (f32[640,128]{1,0:T(8,128)S(1)}, f32[640,128]{1,0:T(8,128)S(1)}, u32[]{:S(2)}, u32[]{:S(2)}) collective-permute-start(f32[640,128]{1,0:T(8,128)S(1)} %bitcast.8), channel_id=1, source_target_pairs={{0,4},{4,0},{8,12},{12,8},{16,20},{20,16},{24,28},{28,24},{32,36},... | collective-permute-start | bytes 983048 | tf_op jit(solution)/shard_map/ppermute | solution.py:78
  66.2 1.7 %collective-permute-start.2 = (f32[4,136,128]{2,1,0:T(8,128)S(1)}, f32[4,136,128]{2,1,0:T(8,128)S(1)}, u32[]{:S(2)}, u32[]{:S(2)}) collective-permute-start(f32[4,136,128]{2,1,0:T(8,128)S(1)} %get-tuple-element.11), channel_id=1, source_target_pairs={{0,4},{4,0},{8,12},{12,8},{16,20},{20,16},{24,28},{28,24},{32,36},... | collective-permute-start | bytes 835592 | tf_op jit(solution)/shard_map/ppermute | solution.py:78
  68.9 13.9 %all-to-all-start.2 = ((bf16[32,24,128]{2,1,0:T(8,128)(2,1)}), bf16[32,24,128]{2,1,0:T(8,128)(2,1)S(1)}, u32[]{:S(2)}, u32[]{:S(2)}) async-start(bf16[32,24,128]{2,1,0:T(8,128)(2,1)} %shard_map.70), calls=%async_computation.2 | async-start | bytes 393216 | tf_op jit(solution)/shard_map/all_to_all | solution.py:82
  97.6 3.8 %collective-permute-start.3 = (bf16[32,16,128]{2,1,0:T(8,128)(2,1)S(1)}, bf16[32,16,128]{2,1,0:T(8,128)(2,1)S(1)}, u32[]{:S(2)}, u32[]{:S(2)}) collective-permute-start(bf16[32,16,128]{2,1,0:T(8,128)(2,1)S(1)} %all_to_all.22.near_ref), channel_id=1, source_target_pairs={{0,4},{4,0},{8,12},{12,8},{16,20},{20,16},{24,28},{28,24},{32,36},... | collective-permute-start | bytes 393224 | tf_op jit(solution)/shard_map/ppermute | solution.py:78

commit v2 on v1

--- a/solution.py
+++ b/solution.py
@@ -201,7 +201,7 @@
     return out
 
 
-def find_basis(core_ref, near_ref, far_ref, basis_ref, power_ref, work_ref):
+def find_basis(core_ref, near_ref, far_ref, basis_ref, power_ref, work_ref, arrivals):
     for at in range(KV_HEADS):
         group = jnp.bitwise_xor(core_ref[0] * HALF, at)
         lanes = pl.ds(pl.multiple_of(group * HEAD_DIM, HEAD_DIM), HEAD_DIM)
@@ -212,6 +212,8 @@
     cross = nt(high, middle) + nt(high, low)
     gram = nt(high, high) + (nt(middle, middle) + (cross + cross.T))
     inverse = factor_inverse(gram, work_ref)
+    for arrival in arrivals:
+        arrival.wait()
     first, second = split(inverse, 2), (high, middle)
     left = jnp.concatenate([first[0], first[0], first[1]], axis=1)
     right = jnp.concatenate([second[0], second[1], second[0]], axis=0)
@@ -252,16 +254,12 @@
     row = lax.broadcasted_iota(jnp.int32, (STACKED, QUERIES), 0)
     lane = lax.broadcasted_iota(jnp.int32, (STACKED, QUERIES), 1)
     own_mask = jnp.where(row % QUERIES == lane, 1.0, 0.0).astype(jnp.bfloat16)
-    find_basis(core_ref, near_ref, far_ref, basis_ref, power_ref, work_ref)
-    copies[0].wait()
-    for lo in range(0, positions, positions // 4):
-        hi = lo + positions // 4
-        rank = nt(basis_ref[...], keys_buf[lo:hi, :])
-        masked_ref[:RANK, lo:hi] = rank.astype(jnp.bfloat16)
-    copies[2].start()
-    lane = lax.broadcasted_iota(jnp.int32, (STACKED, HEAD_DIM), 1)
-    for half, out_ref in enumerate((send_ref, keep_ref)):
-        start = jnp.bitwise_xor(core_ref[0], 1 - half) * HALF
+    for half in range(NC):
+        for at in range(HALF):
+            projected_ref[half, at * STACKED : (at + 1) * STACKED, RANK:] = own_mask
+    find_basis(core_ref, near_ref, far_ref, basis_ref, power_ref, work_ref, copies[:2])
+    starts = [jnp.bitwise_xor(core_ref[0], 1) * HALF, core_ref[0] * HALF]
+    for half, start in enumerate(starts):
         for at in range(HALF):
             g = start + at
             stacked = []
@@ -270,27 +268,38 @@
                 stacked.append(queries_ref[:, own])
             stacked = jnp.concatenate(stacked, axis=0)
             lanes = pl.ds(pl.multiple_of(g * HEAD_DIM, HEAD_DIM), HEAD_DIM)
-            rows = slice(at * STACKED, (at + 1) * STACKED)
             projected = nt(stacked, basis_ref[:, lanes]).astype(jnp.bfloat16)
-            projected_ref[half, rows, :RANK] = projected
-            projected_ref[half, rows, RANK:] = own_mask
-        for lo in range(0, positions, positions // 4):
-            hi = lo + positions // 4
-            scores_ref[half, :, lo:hi] = nn(projected_ref[half], masked_ref[:, lo:hi])
-        if half == 0:
-            copies[1].wait()
+            projected_ref[half, at * STACKED : (at + 1) * STACKED, :RANK] = projected
+    block = positions // 4
+    for lo in range(0, positions, block):
+        rank = nt(basis_ref[...], keys_buf[lo : lo + block, :])
+        masked_ref[:RANK, lo : lo + block] = rank.astype(jnp.bfloat16)
+
+    def score(half):
+        tops = None
+        for lo in range(0, positions, block):
+            scores = nn(projected_ref[half], masked_ref[:, lo : lo + block])
+            scores_ref[half, :, lo : lo + block] = scores
+            for i in range(0, block, HEAD_DIM):
+                piece = scores[:, i : i + HEAD_DIM]
+                tops = piece if tops is None else jnp.maximum(tops, piece)
+        return jnp.max(tops, axis=1, keepdims=True)
+
+    lane = lax.broadcasted_iota(jnp.int32, (STACKED, HEAD_DIM), 1)
+
+    def finish(half, tops, out_ref):
         extras = jnp.zeros((STACKED, HEAD_DIM), jnp.float32)
         for pair in range(0, HALF, 2):
             weights = []
             for at in (pair, pair + 1):
-                scores = scores_ref[half, at * STACKED : (at + 1) * STACKED, :]
-                top = jnp.max(scores, axis=1, keepdims=True)
-                expo = jnp.exp2((scores - top) * LOG_SCALE)
+                rows = slice(at * STACKED, (at + 1) * STACKED)
+                expo = jnp.exp2((scores_ref[half, rows, :] - tops[rows]) * LOG_SCALE)
                 total = jnp.sum(expo, axis=1, keepdims=True)
                 weights.append(expo.astype(jnp.bfloat16))
-                extras = jnp.where(lane == 2 * at, top * LOG_SCALE, extras)
+                extras = jnp.where(lane == 2 * at, tops[rows] * LOG_SCALE, extras)
                 extras = jnp.where(lane == 2 * at + 1, total, extras)
-            lanes = pl.ds(pl.multiple_of((start + pair) * HEAD_DIM, 2 * HEAD_DIM), 2 * HEAD_DIM)
+            first = (starts[half] + pair) * HEAD_DIM
+            lanes = pl.ds(pl.multiple_of(first, 2 * HEAD_DIM), 2 * HEAD_DIM)
             both = nn(jnp.concatenate(weights, axis=0), values_buf[:, lanes])
             out_ref[pair, :STACKED, :] = both[:STACKED, :HEAD_DIM]
             out_ref[pair + 1, :STACKED, :] = both[STACKED:, HEAD_DIM:]
@@ -298,6 +307,11 @@
         for at in range(HALF):
             row = extras[2 * at : 2 * at + 2]
             out_ref[at, STACKED:, :] = jnp.concatenate([row] * (EXTRA // 2), axis=0)
+
+    tops = [score(half) for half in range(NC)]
+    finish(0, tops[0], send_ref)
+    copies[2].start()
+    finish(1, tops[1], keep_ref)
     copies[2].wait()
 
 

time: 103 us -> 104 us (level)
  Pallas kernels: 20.2 us -> 21.3 us
    pallas_call x1, Pallas kernels: 13.3 us -> 14.4 us  [attend(): pl.pallas_call(attend_kernel, out_shape=[jax.ShapeDtypeStruct((RANK, posi...]
where the time goes in v2:
time: 104 us; the launch traced here: 103 us
  blocking collectives  51.4 us (49%)
  Pallas kernels  21.3 us (20%)
  starting transfers between devices  15.7 us (15%)
  waiting for transfers between devices  14 us (13%)
    all_to_all x3, blocking collectives, scatter(): return lax.all_to_all(x, 'ctx', 0, 0, axis_index_groups=CORES)  51.4 us
    pallas_call x1, Pallas kernels, attend(): pl.pallas_call(attend_kernel, out_shape=[jax.ShapeDtypeStruct((RANK, posi...  14.4 us
    ppermute x4, starting transfers between devices, across(): return lax.ppermute(x, 'ctx', pairs)  11.1 us
    all_to_all x1, waiting for transfers between devices, scatter(): return lax.all_to_all(x, 'ctx', 0, 0, axis_index_groups=CORES)  9.36 us
    pallas_call x1, Pallas kernels, local_power(): pl.pallas_call(lambda *refs: power_kernel(*refs, pieces=pieces), in_specs...  4.76 us
    ppermute x4, waiting for transfers between devices, across(): return lax.ppermute(x, 'ctx', pairs)  4.59 us
    all_to_all x1, starting transfers between devices, scatter(): return lax.all_to_all(x, 'ctx', 0, 0, axis_index_groups=CORES)  4.51 us
  transfers between devices with their start and end apart: 5, of which 5 were waited for; matrix products, arithmetic and copies ran while one was open for 0% of the time, Pallas kernels for 0%

profile of v2, /device:TPU:1, one launch (start us, length us, event | category | flops | bytes accessed | tf_op | source)
XLA Modules:
  0.0 103.3 jit_solution(13908699802528412981)
XLA Ops:
  0.6 0.0 copy-start.1
  0.6 0.0 copy-start
  0.7 4.8 %shard_map.68 = (f32[640,128]{1,0:T(8,128)S(1)}, f32[640,128]{1,0:T(8,128)S(1)}) custom-call(s32[1]{0:T(128)} %bitcast.refs_0_.core_ref, bf16[2048,1024]{1,0:T(8,128)(2,1)} %keys_ref.1, bf16[160,1024]{1,0:T(8,128)(2,1)} %bitcast.12), custom_call_target="tpu_custom_call" | custom-call | tf_op jit(solution)/shard_map/pallas_call | solution.py:126
  5.4 3.3 %collective-permute-start = (f32[640,128]{1,0:T(8,128)S(1)}, f32[640,128]{1,0:T(8,128)S(1)}, u32[]{:S(2)}, u32[]{:S(2)}) collective-permute-start(f32[640,128]{1,0:T(8,128)S(1)} %get-tuple-element.8), channel_id=1, source_target_pairs={{0,4},{4,0},{8,12},{12,8},{16,20},{20,16},{24,28},{28,24},{32,36},... | collective-permute-start | bytes 983048 | tf_op jit(solution)/shard_map/ppermute | solution.py:78
  8.8 1.3 %collective-permute-done = f32[640,128]{1,0:T(8,128)S(1)} collective-permute-done((f32[640,128]{1,0:T(8,128)S(1)}, f32[640,128]{1,0:T(8,128)S(1)}, u32[]{:S(2)}, u32[]{:S(2)}) %collective-permute-start) | collective-permute-done | bytes 327712 | tf_op jit(solution)/shard_map/ppermute | solution.py:78
  10.0 19.7 %all_to_all.20 = f32[32,5,4,128]{3,2,1,0:T(4,128)S(1)} all-to-all(f32[32,5,4,128]{3,2,1,0:T(4,128)S(1)} %bitcast.11), channel_id=1, replica_groups={{0,8,16,24,32,40,48,56,64,72,80,88,96,104,112,120,128,136,144,152,160,1..., dimensions={0} | all-to-all | bytes 655360 | tf_op jit(solution)/shard_map/all_to_all | solution.py:82
  29.8 0.1 reduce_sum.9
  29.9 17.3 %all_to_all.21 = f32[32,5,4,128]{3,2,1,0:T(4,128)S(1)} all-to-all(f32[32,5,4,128]{3,2,1,0:T(4,128)S(1)} %broadcast_in_dim.6), channel_id=1, replica_groups={{0,8,16,24,32,40,48,56,64,72,80,88,96,104,112,120,128,136,144,152,160,1..., dimensions={0} | all-to-all | bytes 655360 | tf_op jit(solution)/shard_map/all_to_all | solution.py:82
  47.2 4.5 %collective-permute-start.1 = (f32[640,128]{1,0:T(8,128)S(1)}, f32[640,128]{1,0:T(8,128)S(1)}, u32[]{:S(2)}, u32[]{:S(2)}) collective-permute-start(f32[640,128]{1,0:T(8,128)S(1)} %bitcast.8), channel_id=1, source_target_pairs={{0,4},{4,0},{8,12},{12,8},{16,20},{20,16},{24,28},{28,24},{32,36},... | collective-permute-start | bytes 983048 | tf_op jit(solution)/shard_map/ppermute | solution.py:78
  51.6 0.0 copy-done.1
  51.6 0.1 sub.16.limit_ref
  51.7 1.2 %collective-permute-done.1.far_ref = f32[640,128]{1,0:T(8,128)S(1)} collective-permute-done((f32[640,128]{1,0:T(8,128)S(1)}, f32[640,128]{1,0:T(8,128)S(1)}, u32[]{:S(2)}, u32[]{:S(2)}) %collective-permute-start.1) | collective-permute-done | bytes 327712 | tf_op jit(solution)/shard_map/ppermute | solution.py:78
  52.9 0.0 copy-done
  52.9 14.4 %shard_map.69 = (bf16[160,2048]{1,0:T(8,128)(2,1)}, f32[4,136,128]{2,1,0:T(8,128)S(1)}, f32[4,136,128]{2,1,0:T(8,128)S(1)}) custom-call(s32[1]{0:T(128)} %bitcast.refs_0_.core_ref, f32[640,128]{1,0:T(8,128)S(1)} %bitcast.9, f32[640,128]{1,0:T(8,128)S(1)} %collective-permute-done.1.far_ref, bf16[2048,1024]{1,0:T(8,128)(2,1)} %keys_ref.1, ...), custom_call_target="tpu_custom_call" | custom-call | tf_op jit(solution)/shard_map/pallas_call | solution.py:320
  67.3 0.5 collective-permute-start.2
  67.8 1.2 %collective-permute-done.2.sent_ref = f32[4,136,128]{2,1,0:T(8,128)S(1)} collective-permute-done((f32[4,136,128]{2,1,0:T(8,128)S(1)}, f32[4,136,128]{2,1,0:T(8,128)S(1)}, u32[]{:S(2)}, u32[]{:S(2)}) %collective-permute-start.2) | collective-permute-done | bytes 278560 | tf_op jit(solution)/shard_map/ppermute | solution.py:78
  69.0 1.0 shard_map.70
  70.0 4.5 %all-to-all-start.2 = ((bf16[32,24,128]{2,1,0:T(8,128)(2,1)}), bf16[32,24,128]{2,1,0:T(8,128)(2,1)S(1)}, u32[]{:S(2)}, u32[]{:S(2)}) async-start(bf16[32,24,128]{2,1,0:T(8,128)(2,1)} %shard_map.70), calls=%async_computation.2 | async-start | bytes 393216 | tf_op jit(solution)/shard_map/all_to_all | solution.py:82
  74.6 9.4 %all-to-all-done.2.parts_ref = bf16[32,24,128]{2,1,0:T(8,128)(2,1)S(1)} async-done(((bf16[32,24,128]{2,1,0:T(8,128)(2,1)}), bf16[32,24,128]{2,1,0:T(8,128)(2,1)S(1)}, u32[]{:S(2)}, u32[]{:S(2)}) %all-to-all-start.2) | async-done | bytes 196640 | tf_op jit(solution)/shard_map/all_to_all | solution.py:82
  84.0 0.4 shard_map.71
  84.3 14.4 %all_to_all.22.near_ref = bf16[32,16,128]{2,1,0:T(8,128)(2,1)S(1)} all-to-all(bf16[32,16,128]{2,1,0:T(8,128)(2,1)S(1)} %broadcast_in_dim.7), channel_id=1, replica_groups={{0,8,16,24,32,40,48,56,64,72,80,88,96,104,112,120,128,136,144,152,160,1..., dimensions={0} | all-to-all | bytes 262144 | tf_op jit(solution)/shard_map/all_to_all | solution.py:82
  98.7 2.9 %collective-permute-start.3 = (bf16[32,16,128]{2,1,0:T(8,128)(2,1)S(1)}, bf16[32,16,128]{2,1,0:T(8,128)(2,1)S(1)}, u32[]{:S(2)}, u32[]{:S(2)}) collective-permute-start(bf16[32,16,128]{2,1,0:T(8,128)(2,1)S(1)} %all_to_all.22.near_ref), channel_id=1, source_target_pairs={{0,4},{4,0},{8,12},{12,8},{16,20},{20,16},{24,28},{28,24},{32,36},... | collective-permute-start | bytes 393224 | tf_op jit(solution)/shard_map/ppermute | solution.py:78
  101.6 1.0 collective-permute-done.3.far_ref
  102.6 0.8 shard_map.72
  (4 shorter events, 0.1 us)
Async XLA Ops:
  0.6 51.0 %copy-start.1 = (s32[2,16]{1,0:T(2,128)S(1)}, s32[2,16]{1,0:T(2,128)}, u32[]{:S(2)}) copy-start(s32[2,16]{1,0:T(2,128)} %param.9) | copy-start | bytes 388
  0.6 52.3 %copy-start = (bf16[2,16,4096]{2,1,0:T(8,128)(2,1)S(1)}, bf16[2,16,4096]{2,1,0:T(8,128)(2,1)}, u32[]{:S(2)}) copy-start(bf16[2,16,4096]{2,1,0:T(8,128)(2,1)} %param.8) | copy-start | bytes 786436
  5.4 4.6 %collective-permute-start = (f32[640,128]{1,0:T(8,128)S(1)}, f32[640,128]{1,0:T(8,128)S(1)}, u32[]{:S(2)}, u32[]{:S(2)}) collective-permute-start(f32[640,128]{1,0:T(8,128)S(1)} %get-tuple-element.8), channel_id=1, source_target_pairs={{0,4},{4,0},{8,12},{12,8},{16,20},{20,16},{24,28},{28,24},{32,36},... | collective-permute-start | bytes 983048 | tf_op jit(solution)/shard_map/ppermute | solution.py:78
  47.2 5.7 %collective-permute-start.1 = (f32[640,128]{1,0:T(8,128)S(1)}, f32[640,128]{1,0:T(8,128)S(1)}, u32[]{:S(2)}, u32[]{:S(2)}) collective-permute-start(f32[640,128]{1,0:T(8,128)S(1)} %bitcast.8), channel_id=1, source_target_pairs={{0,4},{4,0},{8,12},{12,8},{16,20},{20,16},{24,28},{28,24},{32,36},... | collective-permute-start | bytes 983048 | tf_op jit(solution)/shard_map/ppermute | solution.py:78
  67.3 1.7 %collective-permute-start.2 = (f32[4,136,128]{2,1,0:T(8,128)S(1)}, f32[4,136,128]{2,1,0:T(8,128)S(1)}, u32[]{:S(2)}, u32[]{:S(2)}) collective-permute-start(f32[4,136,128]{2,1,0:T(8,128)S(1)} %get-tuple-element.11), channel_id=1, source_target_pairs={{0,4},{4,0},{8,12},{12,8},{16,20},{20,16},{24,28},{28,24},{32,36},... | collective-permute-start | bytes 835592 | tf_op jit(solution)/shard_map/ppermute | solution.py:78
  70.0 13.9 %all-to-all-start.2 = ((bf16[32,24,128]{2,1,0:T(8,128)(2,1)}), bf16[32,24,128]{2,1,0:T(8,128)(2,1)S(1)}, u32[]{:S(2)}, u32[]{:S(2)}) async-start(bf16[32,24,128]{2,1,0:T(8,128)(2,1)} %shard_map.70), calls=%async_computation.2 | async-start | bytes 393216 | tf_op jit(solution)/shard_map/all_to_all | solution.py:82
  98.7 3.8 %collective-permute-start.3 = (bf16[32,16,128]{2,1,0:T(8,128)(2,1)S(1)}, bf16[32,16,128]{2,1,0:T(8,128)(2,1)S(1)}, u32[]{:S(2)}, u32[]{:S(2)}) collective-permute-start(bf16[32,16,128]{2,1,0:T(8,128)(2,1)S(1)} %all_to_all.22.near_ref), channel_id=1, source_target_pairs={{0,4},{4,0},{8,12},{12,8},{16,20},{20,16},{24,28},{28,24},{32,36},... | collective-permute-start | bytes 393224 | tf_op jit(solution)/shard_map/ppermute | solution.py:78

commit v3 on v1

--- a/solution.py
+++ b/solution.py
@@ -237,6 +237,7 @@
     masked_ref,
     projected_ref,
     scores_ref,
+    weights_ref,
     sems,
 ):
     copies = [
@@ -281,17 +282,25 @@
             copies[1].wait()
         extras = jnp.zeros((STACKED, HEAD_DIM), jnp.float32)
         for pair in range(0, HALF, 2):
-            weights = []
             for at in (pair, pair + 1):
-                scores = scores_ref[half, at * STACKED : (at + 1) * STACKED, :]
-                top = jnp.max(scores, axis=1, keepdims=True)
-                expo = jnp.exp2((scores - top) * LOG_SCALE)
-                total = jnp.sum(expo, axis=1, keepdims=True)
-                weights.append(expo.astype(jnp.bfloat16))
+                rows = slice(at * STACKED, (at + 1) * STACKED)
+                tops = None
+                for lo in range(0, positions, LANES):
+                    piece = scores_ref[half, rows, lo : lo + LANES]
+                    tops = piece if tops is None else jnp.maximum(tops, piece)
+                top = jnp.max(tops, axis=1, keepdims=True)
+                totals = None
+                for lo in range(0, positions, LANES):
+                    piece = scores_ref[half, rows, lo : lo + LANES]
+                    expo = jnp.exp2((piece - top) * LOG_SCALE)
+                    totals = expo if totals is None else totals + expo
+                    weights_ref[half, rows, lo : lo + LANES] = expo.astype(jnp.bfloat16)
+                total = jnp.sum(totals, axis=1, keepdims=True)
                 extras = jnp.where(lane == 2 * at, top * LOG_SCALE, extras)
                 extras = jnp.where(lane == 2 * at + 1, total, extras)
             lanes = pl.ds(pl.multiple_of((start + pair) * HEAD_DIM, 2 * HEAD_DIM), 2 * HEAD_DIM)
-            both = nn(jnp.concatenate(weights, axis=0), values_buf[:, lanes])
+            rows = slice(pair * STACKED, (pair + 2) * STACKED)
+            both = nn(weights_ref[half, rows, :], values_buf[:, lanes])
             out_ref[pair, :STACKED, :] = both[:STACKED, :HEAD_DIM]
             out_ref[pair + 1, :STACKED, :] = both[STACKED:, HEAD_DIM:]
         extras = extras.T
@@ -320,6 +329,7 @@
             pltpu.VMEM((RANK + QUERIES, positions), jnp.bfloat16),
             pltpu.VMEM((NC, HALF * STACKED, RANK + QUERIES), jnp.bfloat16),
             pltpu.VMEM((NC, HALF * STACKED, positions), jnp.float32),
+            pltpu.VMEM((NC, HALF * STACKED, positions), jnp.bfloat16),
             pltpu.SemaphoreType.DMA((3,)),
         ],
         compiler_params=params(),

time: 103 us -> 103 us (level)
  no operation moved by 1% of the time
where the time goes in v3:
time: 103 us
  blocking collectives  51.4 us (50%)
  Pallas kernels  20.9 us (20%)
  starting transfers between devices  15.6 us (15%)
  waiting for transfers between devices  14 us (14%)
    all_to_all x3, blocking collectives, scatter(): return lax.all_to_all(x, 'ctx', 0, 0, axis_index_groups=CORES)  51.4 us
    pallas_call x1, Pallas kernels, attend(): pl.pallas_call(attend_kernel, out_shape=[jax.ShapeDtypeStruct((RANK, posi...  14 us
    ppermute x4, starting transfers between devices, across(): return lax.ppermute(x, 'ctx', pairs)  11.1 us
    all_to_all x1, waiting for transfers between devices, scatter(): return lax.all_to_all(x, 'ctx', 0, 0, axis_index_groups=CORES)  9.36 us
    pallas_call x1, Pallas kernels, local_power(): pl.pallas_call(lambda *refs: power_kernel(*refs, pieces=pieces), in_specs...  4.75 us
    ppermute x4, waiting for transfers between devices, across(): return lax.ppermute(x, 'ctx', pairs)  4.6 us
    all_to_all x1, starting transfers between devices, scatter(): return lax.all_to_all(x, 'ctx', 0, 0, axis_index_groups=CORES)  4.52 us
  transfers between devices with their start and end apart: 5, of which 5 were waited for; matrix products, arithmetic and copies ran while one was open for 0% of the time, Pallas kernels for 0%

profile of v3, /device:TPU:1, one launch (start us, length us, event | category | flops | bytes accessed | tf_op | source)
XLA Modules:
  0.0 102.9 jit_solution(453166115948869725)
XLA Ops:
  0.6 0.0 copy-start.1
  0.6 0.0 copy-start
  0.7 4.8 %shard_map.68 = (f32[640,128]{1,0:T(8,128)S(1)}, f32[640,128]{1,0:T(8,128)S(1)}) custom-call(s32[1]{0:T(128)} %bitcast.refs_0_.core_ref, bf16[2048,1024]{1,0:T(8,128)(2,1)} %keys_ref.1, bf16[160,1024]{1,0:T(8,128)(2,1)} %bitcast.12), custom_call_target="tpu_custom_call" | custom-call | tf_op jit(solution)/shard_map/pallas_call | solution.py:126
  5.4 3.3 %collective-permute-start = (f32[640,128]{1,0:T(8,128)S(1)}, f32[640,128]{1,0:T(8,128)S(1)}, u32[]{:S(2)}, u32[]{:S(2)}) collective-permute-start(f32[640,128]{1,0:T(8,128)S(1)} %get-tuple-element.8), channel_id=1, source_target_pairs={{0,4},{4,0},{8,12},{12,8},{16,20},{20,16},{24,28},{28,24},{32,36},... | collective-permute-start | bytes 983048 | tf_op jit(solution)/shard_map/ppermute | solution.py:78
  8.8 1.3 %collective-permute-done = f32[640,128]{1,0:T(8,128)S(1)} collective-permute-done((f32[640,128]{1,0:T(8,128)S(1)}, f32[640,128]{1,0:T(8,128)S(1)}, u32[]{:S(2)}, u32[]{:S(2)}) %collective-permute-start) | collective-permute-done | bytes 327712 | tf_op jit(solution)/shard_map/ppermute | solution.py:78
  10.0 19.7 %all_to_all.20 = f32[32,5,4,128]{3,2,1,0:T(4,128)S(1)} all-to-all(f32[32,5,4,128]{3,2,1,0:T(4,128)S(1)} %bitcast.11), channel_id=1, replica_groups={{0,8,16,24,32,40,48,56,64,72,80,88,96,104,112,120,128,136,144,152,160,1..., dimensions={0} | all-to-all | bytes 655360 | tf_op jit(solution)/shard_map/all_to_all | solution.py:82
  29.8 0.1 reduce_sum.9
  29.9 17.3 %all_to_all.21 = f32[32,5,4,128]{3,2,1,0:T(4,128)S(1)} all-to-all(f32[32,5,4,128]{3,2,1,0:T(4,128)S(1)} %broadcast_in_dim.6), channel_id=1, replica_groups={{0,8,16,24,32,40,48,56,64,72,80,88,96,104,112,120,128,136,144,152,160,1..., dimensions={0} | all-to-all | bytes 655360 | tf_op jit(solution)/shard_map/all_to_all | solution.py:82
  47.2 4.5 %collective-permute-start.1 = (f32[640,128]{1,0:T(8,128)S(1)}, f32[640,128]{1,0:T(8,128)S(1)}, u32[]{:S(2)}, u32[]{:S(2)}) collective-permute-start(f32[640,128]{1,0:T(8,128)S(1)} %bitcast.8), channel_id=1, source_target_pairs={{0,4},{4,0},{8,12},{12,8},{16,20},{20,16},{24,28},{28,24},{32,36},... | collective-permute-start | bytes 983048 | tf_op jit(solution)/shard_map/ppermute | solution.py:78
  51.6 0.0 copy-done.1
  51.6 0.1 sub.16.limit_ref
  51.7 1.2 %collective-permute-done.1.far_ref = f32[640,128]{1,0:T(8,128)S(1)} collective-permute-done((f32[640,128]{1,0:T(8,128)S(1)}, f32[640,128]{1,0:T(8,128)S(1)}, u32[]{:S(2)}, u32[]{:S(2)}) %collective-permute-start.1) | collective-permute-done | bytes 327712 | tf_op jit(solution)/shard_map/ppermute | solution.py:78
  52.9 0.0 copy-done
  52.9 14.0 %shard_map.69 = (bf16[160,2048]{1,0:T(8,128)(2,1)}, f32[4,136,128]{2,1,0:T(8,128)S(1)}, f32[4,136,128]{2,1,0:T(8,128)S(1)}) custom-call(s32[1]{0:T(128)} %bitcast.refs_0_.core_ref, f32[640,128]{1,0:T(8,128)S(1)} %bitcast.9, f32[640,128]{1,0:T(8,128)S(1)} %collective-permute-done.1.far_ref, bf16[2048,1024]{1,0:T(8,128)(2,1)} %keys_ref.1, ...), custom_call_target="tpu_custom_call" | custom-call | tf_op jit(solution)/shard_map/pallas_call | solution.py:315
  66.9 0.5 collective-permute-start.2
  67.4 1.2 %collective-permute-done.2.sent_ref = f32[4,136,128]{2,1,0:T(8,128)S(1)} collective-permute-done((f32[4,136,128]{2,1,0:T(8,128)S(1)}, f32[4,136,128]{2,1,0:T(8,128)S(1)}, u32[]{:S(2)}, u32[]{:S(2)}) %collective-permute-start.2) | collective-permute-done | bytes 278560 | tf_op jit(solution)/shard_map/ppermute | solution.py:78
  68.6 1.0 shard_map.70
  69.6 4.5 %all-to-all-start.2 = ((bf16[32,24,128]{2,1,0:T(8,128)(2,1)}), bf16[32,24,128]{2,1,0:T(8,128)(2,1)S(1)}, u32[]{:S(2)}, u32[]{:S(2)}) async-start(bf16[32,24,128]{2,1,0:T(8,128)(2,1)} %shard_map.70), calls=%async_computation.2 | async-start | bytes 393216 | tf_op jit(solution)/shard_map/all_to_all | solution.py:82
  74.2 9.4 %all-to-all-done.2.parts_ref = bf16[32,24,128]{2,1,0:T(8,128)(2,1)S(1)} async-done(((bf16[32,24,128]{2,1,0:T(8,128)(2,1)}), bf16[32,24,128]{2,1,0:T(8,128)(2,1)S(1)}, u32[]{:S(2)}, u32[]{:S(2)}) %all-to-all-start.2) | async-done | bytes 196640 | tf_op jit(solution)/shard_map/all_to_all | solution.py:82
  83.5 0.4 shard_map.71
  83.9 14.4 %all_to_all.22.near_ref = bf16[32,16,128]{2,1,0:T(8,128)(2,1)S(1)} all-to-all(bf16[32,16,128]{2,1,0:T(8,128)(2,1)S(1)} %broadcast_in_dim.7), channel_id=1, replica_groups={{0,8,16,24,32,40,48,56,64,72,80,88,96,104,112,120,128,136,144,152,160,1..., dimensions={0} | all-to-all | bytes 262144 | tf_op jit(solution)/shard_map/all_to_all | solution.py:82
  98.3 2.9 %collective-permute-start.3 = (bf16[32,16,128]{2,1,0:T(8,128)(2,1)S(1)}, bf16[32,16,128]{2,1,0:T(8,128)(2,1)S(1)}, u32[]{:S(2)}, u32[]{:S(2)}) collective-permute-start(bf16[32,16,128]{2,1,0:T(8,128)(2,1)S(1)} %all_to_all.22.near_ref), channel_id=1, source_target_pairs={{0,4},{4,0},{8,12},{12,8},{16,20},{20,16},{24,28},{28,24},{32,36},... | collective-permute-start | bytes 393224 | tf_op jit(solution)/shard_map/ppermute | solution.py:78
  101.2 1.0 collective-permute-done.3.far_ref
  102.2 0.8 shard_map.72
  (4 shorter events, 0.1 us)
Async XLA Ops:
  0.6 51.0 %copy-start.1 = (s32[2,16]{1,0:T(2,128)S(1)}, s32[2,16]{1,0:T(2,128)}, u32[]{:S(2)}) copy-start(s32[2,16]{1,0:T(2,128)} %param.9) | copy-start | bytes 388
  0.6 52.3 %copy-start = (bf16[2,16,4096]{2,1,0:T(8,128)(2,1)S(1)}, bf16[2,16,4096]{2,1,0:T(8,128)(2,1)}, u32[]{:S(2)}) copy-start(bf16[2,16,4096]{2,1,0:T(8,128)(2,1)} %param.8) | copy-start | bytes 786436
  5.4 4.6 %collective-permute-start = (f32[640,128]{1,0:T(8,128)S(1)}, f32[640,128]{1,0:T(8,128)S(1)}, u32[]{:S(2)}, u32[]{:S(2)}) collective-permute-start(f32[640,128]{1,0:T(8,128)S(1)} %get-tuple-element.8), channel_id=1, source_target_pairs={{0,4},{4,0},{8,12},{12,8},{16,20},{20,16},{24,28},{28,24},{32,36},... | collective-permute-start | bytes 983048 | tf_op jit(solution)/shard_map/ppermute | solution.py:78
  47.2 5.7 %collective-permute-start.1 = (f32[640,128]{1,0:T(8,128)S(1)}, f32[640,128]{1,0:T(8,128)S(1)}, u32[]{:S(2)}, u32[]{:S(2)}) collective-permute-start(f32[640,128]{1,0:T(8,128)S(1)} %bitcast.8), channel_id=1, source_target_pairs={{0,4},{4,0},{8,12},{12,8},{16,20},{20,16},{24,28},{28,24},{32,36},... | collective-permute-start | bytes 983048 | tf_op jit(solution)/shard_map/ppermute | solution.py:78
  66.9 1.6 %collective-permute-start.2 = (f32[4,136,128]{2,1,0:T(8,128)S(1)}, f32[4,136,128]{2,1,0:T(8,128)S(1)}, u32[]{:S(2)}, u32[]{:S(2)}) collective-permute-start(f32[4,136,128]{2,1,0:T(8,128)S(1)} %get-tuple-element.11), channel_id=1, source_target_pairs={{0,4},{4,0},{8,12},{12,8},{16,20},{20,16},{24,28},{28,24},{32,36},... | collective-permute-start | bytes 835592 | tf_op jit(solution)/shard_map/ppermute | solution.py:78
  69.6 13.9 %all-to-all-start.2 = ((bf16[32,24,128]{2,1,0:T(8,128)(2,1)}), bf16[32,24,128]{2,1,0:T(8,128)(2,1)S(1)}, u32[]{:S(2)}, u32[]{:S(2)}) async-start(bf16[32,24,128]{2,1,0:T(8,128)(2,1)} %shard_map.70), calls=%async_computation.2 | async-start | bytes 393216 | tf_op jit(solution)/shard_map/all_to_all | solution.py:82
  98.3 3.8 %collective-permute-start.3 = (bf16[32,16,128]{2,1,0:T(8,128)(2,1)S(1)}, bf16[32,16,128]{2,1,0:T(8,128)(2,1)S(1)}, u32[]{:S(2)}, u32[]{:S(2)}) collective-permute-start(bf16[32,16,128]{2,1,0:T(8,128)(2,1)S(1)} %all_to_all.22.near_ref), channel_id=1, source_target_pairs={{0,4},{4,0},{8,12},{12,8},{16,20},{20,16},{24,28},{28,24},{32,36},... | collective-permute-start | bytes 393224 | tf_op jit(solution)/shard_map/ppermute | solution.py:78

commit v4 on v1

--- a/solution.py
+++ b/solution.py
@@ -155,7 +155,8 @@
         ]
         for j in range(PANEL):
             ratio = columns[j] * (1.0 / columns[j][j : j + 1])
-            ratio = jnp.where(below[: BLOCK - panel] > j, ratio, 0.0)
+            top = jnp.where(below[:PANEL] > j, ratio[:PANEL], 0.0)
+            ratio = jnp.concatenate([top, ratio[PANEL:]], axis=0) if panel + PANEL < BLOCK else top
             for m in range(j + 1, PANEL):
                 columns[m] = columns[m] - ratio * columns[m][j : j + 1]
             tiles = [tile - ratio * tile[j : j + 1] for tile in tiles]
@@ -201,7 +202,7 @@
     return out
 
 
-def find_basis(core_ref, near_ref, far_ref, basis_ref, power_ref, work_ref):
+def find_basis(core_ref, near_ref, far_ref, basis_ref, power_ref, work_ref, arrivals):
     for at in range(KV_HEADS):
         group = jnp.bitwise_xor(core_ref[0] * HALF, at)
         lanes = pl.ds(pl.multiple_of(group * HEAD_DIM, HEAD_DIM), HEAD_DIM)
@@ -212,6 +213,8 @@
     cross = nt(high, middle) + nt(high, low)
     gram = nt(high, high) + (nt(middle, middle) + (cross + cross.T))
     inverse = factor_inverse(gram, work_ref)
+    for arrival in arrivals:
+        arrival.wait()
     first, second = split(inverse, 2), (high, middle)
     left = jnp.concatenate([first[0], first[0], first[1]], axis=1)
     right = jnp.concatenate([second[0], second[1], second[0]], axis=0)
@@ -252,8 +255,7 @@
     row = lax.broadcasted_iota(jnp.int32, (STACKED, QUERIES), 0)
     lane = lax.broadcasted_iota(jnp.int32, (STACKED, QUERIES), 1)
     own_mask = jnp.where(row % QUERIES == lane, 1.0, 0.0).astype(jnp.bfloat16)
-    find_basis(core_ref, near_ref, far_ref, basis_ref, power_ref, work_ref)
-    copies[0].wait()
+    find_basis(core_ref, near_ref, far_ref, basis_ref, power_ref, work_ref, copies[:2])
     for lo in range(0, positions, positions // 4):
         hi = lo + positions // 4
         rank = nt(basis_ref[...], keys_buf[lo:hi, :])
@@ -277,8 +279,6 @@
         for lo in range(0, positions, positions // 4):
             hi = lo + positions // 4
             scores_ref[half, :, lo:hi] = nn(projected_ref[half], masked_ref[:, lo:hi])
-        if half == 0:
-            copies[1].wait()
         extras = jnp.zeros((STACKED, HEAD_DIM), jnp.float32)
         for pair in range(0, HALF, 2):
             weights = []

time: 103 us -> 103 us (level)
  no operation moved by 1% of the time
where the time goes in v4:
time: 103 us
  blocking collectives  51.4 us (50%)
  Pallas kernels  21.1 us (20%)
  starting transfers between devices  15.6 us (15%)
  waiting for transfers between devices  14 us (14%)
    all_to_all x3, blocking collectives, scatter(): return lax.all_to_all(x, 'ctx', 0, 0, axis_index_groups=CORES)  51.4 us
    pallas_call x1, Pallas kernels, attend(): pl.pallas_call(attend_kernel, out_shape=[jax.ShapeDtypeStruct((RANK, posi...  14.2 us
    ppermute x4, starting transfers between devices, across(): return lax.ppermute(x, 'ctx', pairs)  11.1 us
    all_to_all x1, waiting for transfers between devices, scatter(): return lax.all_to_all(x, 'ctx', 0, 0, axis_index_groups=CORES)  9.36 us
    pallas_call x1, Pallas kernels, local_power(): pl.pallas_call(lambda *refs: power_kernel(*refs, pieces=pieces), in_specs...  4.76 us
    ppermute x4, waiting for transfers between devices, across(): return lax.ppermute(x, 'ctx', pairs)  4.63 us
    all_to_all x1, starting transfers between devices, scatter(): return lax.all_to_all(x, 'ctx', 0, 0, axis_index_groups=CORES)  4.51 us
  transfers between devices with their start and end apart: 5, of which 5 were waited for; matrix products, arithmetic and copies ran while one was open for 0% of the time, Pallas kernels for 0%

profile of v4, /device:TPU:1, one launch (start us, length us, event | category | flops | bytes accessed | tf_op | source)
XLA Modules:
  0.0 103.1 jit_solution(10795542239002705963)
XLA Ops:
  0.6 0.0 copy-start.1
  0.6 0.0 copy-start
  0.7 4.8 %shard_map.68 = (f32[640,128]{1,0:T(8,128)S(1)}, f32[640,128]{1,0:T(8,128)S(1)}) custom-call(s32[1]{0:T(128)} %bitcast.refs_0_.core_ref, bf16[2048,1024]{1,0:T(8,128)(2,1)} %keys_ref.1, bf16[160,1024]{1,0:T(8,128)(2,1)} %bitcast.12), custom_call_target="tpu_custom_call" | custom-call | tf_op jit(solution)/shard_map/pallas_call | solution.py:126
  5.4 3.3 %collective-permute-start = (f32[640,128]{1,0:T(8,128)S(1)}, f32[640,128]{1,0:T(8,128)S(1)}, u32[]{:S(2)}, u32[]{:S(2)}) collective-permute-start(f32[640,128]{1,0:T(8,128)S(1)} %get-tuple-element.8), channel_id=1, source_target_pairs={{0,4},{4,0},{8,12},{12,8},{16,20},{20,16},{24,28},{28,24},{32,36},... | collective-permute-start | bytes 983048 | tf_op jit(solution)/shard_map/ppermute | solution.py:78
  8.8 1.3 %collective-permute-done = f32[640,128]{1,0:T(8,128)S(1)} collective-permute-done((f32[640,128]{1,0:T(8,128)S(1)}, f32[640,128]{1,0:T(8,128)S(1)}, u32[]{:S(2)}, u32[]{:S(2)}) %collective-permute-start) | collective-permute-done | bytes 327712 | tf_op jit(solution)/shard_map/ppermute | solution.py:78
  10.0 19.7 %all_to_all.20 = f32[32,5,4,128]{3,2,1,0:T(4,128)S(1)} all-to-all(f32[32,5,4,128]{3,2,1,0:T(4,128)S(1)} %bitcast.11), channel_id=1, replica_groups={{0,8,16,24,32,40,48,56,64,72,80,88,96,104,112,120,128,136,144,152,160,1..., dimensions={0} | all-to-all | bytes 655360 | tf_op jit(solution)/shard_map/all_to_all | solution.py:82
  29.8 0.1 reduce_sum.9
  29.9 17.3 %all_to_all.21 = f32[32,5,4,128]{3,2,1,0:T(4,128)S(1)} all-to-all(f32[32,5,4,128]{3,2,1,0:T(4,128)S(1)} %broadcast_in_dim.6), channel_id=1, replica_groups={{0,8,16,24,32,40,48,56,64,72,80,88,96,104,112,120,128,136,144,152,160,1..., dimensions={0} | all-to-all | bytes 655360 | tf_op jit(solution)/shard_map/all_to_all | solution.py:82
  47.2 4.5 %collective-permute-start.1 = (f32[640,128]{1,0:T(8,128)S(1)}, f32[640,128]{1,0:T(8,128)S(1)}, u32[]{:S(2)}, u32[]{:S(2)}) collective-permute-start(f32[640,128]{1,0:T(8,128)S(1)} %bitcast.8), channel_id=1, source_target_pairs={{0,4},{4,0},{8,12},{12,8},{16,20},{20,16},{24,28},{28,24},{32,36},... | collective-permute-start | bytes 983048 | tf_op jit(solution)/shard_map/ppermute | solution.py:78
  51.6 0.0 copy-done.1
  51.6 0.1 sub.16.limit_ref
  51.7 1.2 %collective-permute-done.1.far_ref = f32[640,128]{1,0:T(8,128)S(1)} collective-permute-done((f32[640,128]{1,0:T(8,128)S(1)}, f32[640,128]{1,0:T(8,128)S(1)}, u32[]{:S(2)}, u32[]{:S(2)}) %collective-permute-start.1) | collective-permute-done | bytes 327712 | tf_op jit(solution)/shard_map/ppermute | solution.py:78
  52.9 0.0 copy-done
  52.9 14.2 %shard_map.69 = (bf16[160,2048]{1,0:T(8,128)(2,1)}, f32[4,136,128]{2,1,0:T(8,128)S(1)}, f32[4,136,128]{2,1,0:T(8,128)S(1)}) custom-call(s32[1]{0:T(128)} %bitcast.refs_0_.core_ref, f32[640,128]{1,0:T(8,128)S(1)} %bitcast.9, f32[640,128]{1,0:T(8,128)S(1)} %collective-permute-done.1.far_ref, bf16[2048,1024]{1,0:T(8,128)(2,1)} %keys_ref.1, ...), custom_call_target="tpu_custom_call" | custom-call | tf_op jit(solution)/shard_map/pallas_call | solution.py:306
  67.1 0.4 collective-permute-start.2
  67.5 1.2 %collective-permute-done.2.sent_ref = f32[4,136,128]{2,1,0:T(8,128)S(1)} collective-permute-done((f32[4,136,128]{2,1,0:T(8,128)S(1)}, f32[4,136,128]{2,1,0:T(8,128)S(1)}, u32[]{:S(2)}, u32[]{:S(2)}) %collective-permute-start.2) | collective-permute-done | bytes 278560 | tf_op jit(solution)/shard_map/ppermute | solution.py:78
  68.8 1.0 shard_map.70
  69.8 4.5 %all-to-all-start.2 = ((bf16[32,24,128]{2,1,0:T(8,128)(2,1)}), bf16[32,24,128]{2,1,0:T(8,128)(2,1)S(1)}, u32[]{:S(2)}, u32[]{:S(2)}) async-start(bf16[32,24,128]{2,1,0:T(8,128)(2,1)} %shard_map.70), calls=%async_computation.2 | async-start | bytes 393216 | tf_op jit(solution)/shard_map/all_to_all | solution.py:82
  74.3 9.4 %all-to-all-done.2.parts_ref = bf16[32,24,128]{2,1,0:T(8,128)(2,1)S(1)} async-done(((bf16[32,24,128]{2,1,0:T(8,128)(2,1)}), bf16[32,24,128]{2,1,0:T(8,128)(2,1)S(1)}, u32[]{:S(2)}, u32[]{:S(2)}) %all-to-all-start.2) | async-done | bytes 196640 | tf_op jit(solution)/shard_map/all_to_all | solution.py:82
  83.7 0.4 shard_map.71
  84.1 14.4 %all_to_all.22.near_ref = bf16[32,16,128]{2,1,0:T(8,128)(2,1)S(1)} all-to-all(bf16[32,16,128]{2,1,0:T(8,128)(2,1)S(1)} %broadcast_in_dim.7), channel_id=1, replica_groups={{0,8,16,24,32,40,48,56,64,72,80,88,96,104,112,120,128,136,144,152,160,1..., dimensions={0} | all-to-all | bytes 262144 | tf_op jit(solution)/shard_map/all_to_all | solution.py:82
  98.5 2.9 %collective-permute-start.3 = (bf16[32,16,128]{2,1,0:T(8,128)(2,1)S(1)}, bf16[32,16,128]{2,1,0:T(8,128)(2,1)S(1)}, u32[]{:S(2)}, u32[]{:S(2)}) collective-permute-start(bf16[32,16,128]{2,1,0:T(8,128)(2,1)S(1)} %all_to_all.22.near_ref), channel_id=1, source_target_pairs={{0,4},{4,0},{8,12},{12,8},{16,20},{20,16},{24,28},{28,24},{32,36},... | collective-permute-start | bytes 393224 | tf_op jit(solution)/shard_map/ppermute | solution.py:78
  101.4 1.0 collective-permute-done.3.far_ref
  102.3 0.8 shard_map.72
  (4 shorter events, 0.1 us)
Async XLA Ops:
  0.6 51.0 %copy-start.1 = (s32[2,16]{1,0:T(2,128)S(1)}, s32[2,16]{1,0:T(2,128)}, u32[]{:S(2)}) copy-start(s32[2,16]{1,0:T(2,128)} %param.9) | copy-start | bytes 388
  0.6 52.3 %copy-start = (bf16[2,16,4096]{2,1,0:T(8,128)(2,1)S(1)}, bf16[2,16,4096]{2,1,0:T(8,128)(2,1)}, u32[]{:S(2)}) copy-start(bf16[2,16,4096]{2,1,0:T(8,128)(2,1)} %param.8) | copy-start | bytes 786436
  5.4 4.6 %collective-permute-start = (f32[640,128]{1,0:T(8,128)S(1)}, f32[640,128]{1,0:T(8,128)S(1)}, u32[]{:S(2)}, u32[]{:S(2)}) collective-permute-start(f32[640,128]{1,0:T(8,128)S(1)} %get-tuple-element.8), channel_id=1, source_target_pairs={{0,4},{4,0},{8,12},{12,8},{16,20},{20,16},{24,28},{28,24},{32,36},... | collective-permute-start | bytes 983048 | tf_op jit(solution)/shard_map/ppermute | solution.py:78
  47.2 5.7 %collective-permute-start.1 = (f32[640,128]{1,0:T(8,128)S(1)}, f32[640,128]{1,0:T(8,128)S(1)}, u32[]{:S(2)}, u32[]{:S(2)}) collective-permute-start(f32[640,128]{1,0:T(8,128)S(1)} %bitcast.8), channel_id=1, source_target_pairs={{0,4},{4,0},{8,12},{12,8},{16,20},{20,16},{24,28},{28,24},{32,36},... | collective-permute-start | bytes 983048 | tf_op jit(solution)/shard_map/ppermute | solution.py:78
  67.1 1.6 %collective-permute-start.2 = (f32[4,136,128]{2,1,0:T(8,128)S(1)}, f32[4,136,128]{2,1,0:T(8,128)S(1)}, u32[]{:S(2)}, u32[]{:S(2)}) collective-permute-start(f32[4,136,128]{2,1,0:T(8,128)S(1)} %get-tuple-element.11), channel_id=1, source_target_pairs={{0,4},{4,0},{8,12},{12,8},{16,20},{20,16},{24,28},{28,24},{32,36},... | collective-permute-start | bytes 835592 | tf_op jit(solution)/shard_map/ppermute | solution.py:78
  69.8 13.9 %all-to-all-start.2 = ((bf16[32,24,128]{2,1,0:T(8,128)(2,1)}), bf16[32,24,128]{2,1,0:T(8,128)(2,1)S(1)}, u32[]{:S(2)}, u32[]{:S(2)}) async-start(bf16[32,24,128]{2,1,0:T(8,128)(2,1)} %shard_map.70), calls=%async_computation.2 | async-start | bytes 393216 | tf_op jit(solution)/shard_map/all_to_all | solution.py:82
  98.5 3.8 %collective-permute-start.3 = (bf16[32,16,128]{2,1,0:T(8,128)(2,1)S(1)}, bf16[32,16,128]{2,1,0:T(8,128)(2,1)S(1)}, u32[]{:S(2)}, u32[]{:S(2)}) collective-permute-start(bf16[32,16,128]{2,1,0:T(8,128)(2,1)S(1)} %all_to_all.22.near_ref), channel_id=1, source_target_pairs={{0,4},{4,0},{8,12},{12,8},{16,20},{20,16},{24,28},{28,24},{32,36},... | collective-permute-start | bytes 393224 | tf_op jit(solution)/shard_map/ppermute | solution.py:78

commit v5 on v1

--- a/solution.py
+++ b/solution.py
@@ -241,10 +241,17 @@
 ):
     copies = [
         pltpu.make_async_copy(keys_ref, keys_buf, sems.at[0]),
-        pltpu.make_async_copy(values_ref, values_buf, sems.at[1]),
-        pltpu.make_async_copy(masked_ref.at[pl.ds(0, RANK), :], rank_ref, sems.at[2]),
+        pltpu.make_async_copy(masked_ref.at[pl.ds(0, RANK), :], rank_ref, sems.at[1]),
     ]
-    for copy in copies[:2]:
+    for half in range(NC):
+        first = jnp.bitwise_xor(core_ref[0], 1 - half) * HALF * HEAD_DIM
+        lanes = pl.ds(pl.multiple_of(first, HALF * HEAD_DIM), HALF * HEAD_DIM)
+        copies.append(
+            pltpu.make_async_copy(
+                values_ref.at[:, lanes], values_buf.at[:, lanes], sems.at[2 + half]
+            )
+        )
+    for copy in (copies[0], copies[2], copies[3]):
         copy.start()
     positions = keys_buf.shape[0]
     column = lax.broadcasted_iota(jnp.int32, (QUERIES, positions), 1)
@@ -258,7 +265,7 @@
         hi = lo + positions // 4
         rank = nt(basis_ref[...], keys_buf[lo:hi, :])
         masked_ref[:RANK, lo:hi] = rank.astype(jnp.bfloat16)
-    copies[2].start()
+    copies[1].start()
     lane = lax.broadcasted_iota(jnp.int32, (STACKED, HEAD_DIM), 1)
     for half, out_ref in enumerate((send_ref, keep_ref)):
         start = jnp.bitwise_xor(core_ref[0], 1 - half) * HALF
@@ -277,8 +284,7 @@
         for lo in range(0, positions, positions // 4):
             hi = lo + positions // 4
             scores_ref[half, :, lo:hi] = nn(projected_ref[half], masked_ref[:, lo:hi])
-        if half == 0:
-            copies[1].wait()
+        copies[2 + half].wait()
         extras = jnp.zeros((STACKED, HEAD_DIM), jnp.float32)
         for pair in range(0, HALF, 2):
             weights = []
@@ -298,7 +304,7 @@
         for at in range(HALF):
             row = extras[2 * at : 2 * at + 2]
             out_ref[at, STACKED:, :] = jnp.concatenate([row] * (EXTRA // 2), axis=0)
-    copies[2].wait()
+    copies[1].wait()
 
 
 def attend(core, near, far, keys, values, queries, limit):
@@ -320,7 +326,7 @@
             pltpu.VMEM((RANK + QUERIES, positions), jnp.bfloat16),
             pltpu.VMEM((NC, HALF * STACKED, RANK + QUERIES), jnp.bfloat16),
             pltpu.VMEM((NC, HALF * STACKED, positions), jnp.float32),
-            pltpu.SemaphoreType.DMA((3,)),
+            pltpu.SemaphoreType.DMA((4,)),
         ],
         compiler_params=params(),
     )(core, near, far, keys, values, queries, limit)

time: 103 us -> 103 us (level)
  no operation moved by 1% of the time
where the time goes in v5:
time: 103 us; the launch traced here: 102 us
  blocking collectives  51.4 us (50%)
  Pallas kernels  20.4 us (20%)
  starting transfers between devices  15.6 us (15%)
  waiting for transfers between devices  14 us (14%)
    all_to_all x3, blocking collectives, scatter(): return lax.all_to_all(x, 'ctx', 0, 0, axis_index_groups=CORES)  51.4 us
    pallas_call x1, Pallas kernels, attend(): pl.pallas_call(attend_kernel, out_shape=[jax.ShapeDtypeStruct((RANK, posi...  13.5 us
    ppermute x4, starting transfers between devices, across(): return lax.ppermute(x, 'ctx', pairs)  11.1 us
    all_to_all x1, waiting for transfers between devices, scatter(): return lax.all_to_all(x, 'ctx', 0, 0, axis_index_groups=CORES)  9.36 us
    pallas_call x1, Pallas kernels, local_power(): pl.pallas_call(lambda *refs: power_kernel(*refs, pieces=pieces), in_specs...  4.75 us
    ppermute x4, waiting for transfers between devices, across(): return lax.ppermute(x, 'ctx', pairs)  4.59 us
    all_to_all x1, starting transfers between devices, scatter(): return lax.all_to_all(x, 'ctx', 0, 0, axis_index_groups=CORES)  4.51 us
  transfers between devices with their start and end apart: 5, of which 5 were waited for; matrix products, arithmetic and copies ran while one was open for 0% of the time, Pallas kernels for 0%

profile of v5, /device:TPU:1, one launch (start us, length us, event | category | flops | bytes accessed | tf_op | source)
XLA Modules:
  0.0 102.4 jit_solution(15848458062592405936)
XLA Ops:
  0.6 0.0 copy-start.1
  0.6 0.0 copy-start
  0.7 4.8 %shard_map.68 = (f32[640,128]{1,0:T(8,128)S(1)}, f32[640,128]{1,0:T(8,128)S(1)}) custom-call(s32[1]{0:T(128)} %bitcast.refs_0_.core_ref, bf16[2048,1024]{1,0:T(8,128)(2,1)} %keys_ref.1, bf16[160,1024]{1,0:T(8,128)(2,1)} %bitcast.12), custom_call_target="tpu_custom_call" | custom-call | tf_op jit(solution)/shard_map/pallas_call | solution.py:126
  5.4 3.3 %collective-permute-start = (f32[640,128]{1,0:T(8,128)S(1)}, f32[640,128]{1,0:T(8,128)S(1)}, u32[]{:S(2)}, u32[]{:S(2)}) collective-permute-start(f32[640,128]{1,0:T(8,128)S(1)} %get-tuple-element.8), channel_id=1, source_target_pairs={{0,4},{4,0},{8,12},{12,8},{16,20},{20,16},{24,28},{28,24},{32,36},... | collective-permute-start | bytes 983048 | tf_op jit(solution)/shard_map/ppermute | solution.py:78
  8.8 1.3 %collective-permute-done = f32[640,128]{1,0:T(8,128)S(1)} collective-permute-done((f32[640,128]{1,0:T(8,128)S(1)}, f32[640,128]{1,0:T(8,128)S(1)}, u32[]{:S(2)}, u32[]{:S(2)}) %collective-permute-start) | collective-permute-done | bytes 327712 | tf_op jit(solution)/shard_map/ppermute | solution.py:78
  10.0 19.7 %all_to_all.20 = f32[32,5,4,128]{3,2,1,0:T(4,128)S(1)} all-to-all(f32[32,5,4,128]{3,2,1,0:T(4,128)S(1)} %bitcast.11), channel_id=1, replica_groups={{0,8,16,24,32,40,48,56,64,72,80,88,96,104,112,120,128,136,144,152,160,1..., dimensions={0} | all-to-all | bytes 655360 | tf_op jit(solution)/shard_map/all_to_all | solution.py:82
  29.8 0.1 reduce_sum.9
  29.9 17.3 %all_to_all.21 = f32[32,5,4,128]{3,2,1,0:T(4,128)S(1)} all-to-all(f32[32,5,4,128]{3,2,1,0:T(4,128)S(1)} %broadcast_in_dim.6), channel_id=1, replica_groups={{0,8,16,24,32,40,48,56,64,72,80,88,96,104,112,120,128,136,144,152,160,1..., dimensions={0} | all-to-all | bytes 655360 | tf_op jit(solution)/shard_map/all_to_all | solution.py:82
  47.2 4.5 %collective-permute-start.1 = (f32[640,128]{1,0:T(8,128)S(1)}, f32[640,128]{1,0:T(8,128)S(1)}, u32[]{:S(2)}, u32[]{:S(2)}) collective-permute-start(f32[640,128]{1,0:T(8,128)S(1)} %bitcast.8), channel_id=1, source_target_pairs={{0,4},{4,0},{8,12},{12,8},{16,20},{20,16},{24,28},{28,24},{32,36},... | collective-permute-start | bytes 983048 | tf_op jit(solution)/shard_map/ppermute | solution.py:78
  51.6 0.0 copy-done.1
  51.6 0.1 sub.16.limit_ref
  51.7 1.2 %collective-permute-done.1.far_ref = f32[640,128]{1,0:T(8,128)S(1)} collective-permute-done((f32[640,128]{1,0:T(8,128)S(1)}, f32[640,128]{1,0:T(8,128)S(1)}, u32[]{:S(2)}, u32[]{:S(2)}) %collective-permute-start.1) | collective-permute-done | bytes 327712 | tf_op jit(solution)/shard_map/ppermute | solution.py:78
  52.9 0.0 copy-done
  52.9 13.5 %shard_map.69 = (bf16[160,2048]{1,0:T(8,128)(2,1)}, f32[4,136,128]{2,1,0:T(8,128)S(1)}, f32[4,136,128]{2,1,0:T(8,128)S(1)}) custom-call(s32[1]{0:T(128)} %bitcast.refs_0_.core_ref, f32[640,128]{1,0:T(8,128)S(1)} %bitcast.9, f32[640,128]{1,0:T(8,128)S(1)} %collective-permute-done.1.far_ref, bf16[2048,1024]{1,0:T(8,128)(2,1)} %keys_ref.1, ...), custom_call_target="tpu_custom_call" | custom-call | tf_op jit(solution)/shard_map/pallas_call | solution.py:312
  66.4 0.5 collective-permute-start.2
  66.9 1.2 %collective-permute-done.2.sent_ref = f32[4,136,128]{2,1,0:T(8,128)S(1)} collective-permute-done((f32[4,136,128]{2,1,0:T(8,128)S(1)}, f32[4,136,128]{2,1,0:T(8,128)S(1)}, u32[]{:S(2)}, u32[]{:S(2)}) %collective-permute-start.2) | collective-permute-done | bytes 278560 | tf_op jit(solution)/shard_map/ppermute | solution.py:78
  68.1 1.0 %shard_map.70 = bf16[32,24,128]{2,1,0:T(8,128)(2,1)} custom-call(f32[4,136,128]{2,1,0:T(8,128)S(1)} %get-tuple-element.10.keep_ref, f32[4,136,128]{2,1,0:T(8,128)S(1)} %collective-permute-done.2.sent_ref), custom_call_target="tpu_custom_call" | custom-call | tf_op jit(solution)/shard_map/pallas_call | solution.py:367
  69.1 4.5 %all-to-all-start.2 = ((bf16[32,24,128]{2,1,0:T(8,128)(2,1)}), bf16[32,24,128]{2,1,0:T(8,128)(2,1)S(1)}, u32[]{:S(2)}, u32[]{:S(2)}) async-start(bf16[32,24,128]{2,1,0:T(8,128)(2,1)} %shard_map.70), calls=%async_computation.2 | async-start | bytes 393216 | tf_op jit(solution)/shard_map/all_to_all | solution.py:82
  73.6 9.4 %all-to-all-done.2.parts_ref = bf16[32,24,128]{2,1,0:T(8,128)(2,1)S(1)} async-done(((bf16[32,24,128]{2,1,0:T(8,128)(2,1)}), bf16[32,24,128]{2,1,0:T(8,128)(2,1)S(1)}, u32[]{:S(2)}, u32[]{:S(2)}) %all-to-all-start.2) | async-done | bytes 196640 | tf_op jit(solution)/shard_map/all_to_all | solution.py:82
  83.0 0.4 shard_map.71
  83.4 14.4 %all_to_all.22.near_ref = bf16[32,16,128]{2,1,0:T(8,128)(2,1)S(1)} all-to-all(bf16[32,16,128]{2,1,0:T(8,128)(2,1)S(1)} %broadcast_in_dim.7), channel_id=1, replica_groups={{0,8,16,24,32,40,48,56,64,72,80,88,96,104,112,120,128,136,144,152,160,1..., dimensions={0} | all-to-all | bytes 262144 | tf_op jit(solution)/shard_map/all_to_all | solution.py:82
  97.8 2.9 %collective-permute-start.3 = (bf16[32,16,128]{2,1,0:T(8,128)(2,1)S(1)}, bf16[32,16,128]{2,1,0:T(8,128)(2,1)S(1)}, u32[]{:S(2)}, u32[]{:S(2)}) collective-permute-start(bf16[32,16,128]{2,1,0:T(8,128)(2,1)S(1)} %all_to_all.22.near_ref), channel_id=1, source_target_pairs={{0,4},{4,0},{8,12},{12,8},{16,20},{20,16},{24,28},{28,24},{32,36},... | collective-permute-start | bytes 393224 | tf_op jit(solution)/shard_map/ppermute | solution.py:78
  100.6 1.0 collective-permute-done.3.far_ref
  101.6 0.8 shard_map.72
  (4 shorter events, 0.1 us)
Async XLA Ops:
  0.6 51.0 %copy-start.1 = (s32[2,16]{1,0:T(2,128)S(1)}, s32[2,16]{1,0:T(2,128)}, u32[]{:S(2)}) copy-start(s32[2,16]{1,0:T(2,128)} %param.9) | copy-start | bytes 388
  0.6 52.3 %copy-start = (bf16[2,16,4096]{2,1,0:T(8,128)(2,1)S(1)}, bf16[2,16,4096]{2,1,0:T(8,128)(2,1)}, u32[]{:S(2)}) copy-start(bf16[2,16,4096]{2,1,0:T(8,128)(2,1)} %param.8) | copy-start | bytes 786436
  5.4 4.6 %collective-permute-start = (f32[640,128]{1,0:T(8,128)S(1)}, f32[640,128]{1,0:T(8,128)S(1)}, u32[]{:S(2)}, u32[]{:S(2)}) collective-permute-start(f32[640,128]{1,0:T(8,128)S(1)} %get-tuple-element.8), channel_id=1, source_target_pairs={{0,4},{4,0},{8,12},{12,8},{16,20},{20,16},{24,28},{28,24},{32,36},... | collective-permute-start | bytes 983048 | tf_op jit(solution)/shard_map/ppermute | solution.py:78
  47.2 5.7 %collective-permute-start.1 = (f32[640,128]{1,0:T(8,128)S(1)}, f32[640,128]{1,0:T(8,128)S(1)}, u32[]{:S(2)}, u32[]{:S(2)}) collective-permute-start(f32[640,128]{1,0:T(8,128)S(1)} %bitcast.8), channel_id=1, source_target_pairs={{0,4},{4,0},{8,12},{12,8},{16,20},{20,16},{24,28},{28,24},{32,36},... | collective-permute-start | bytes 983048 | tf_op jit(solution)/shard_map/ppermute | solution.py:78
  66.4 1.7 %collective-permute-start.2 = (f32[4,136,128]{2,1,0:T(8,128)S(1)}, f32[4,136,128]{2,1,0:T(8,128)S(1)}, u32[]{:S(2)}, u32[]{:S(2)}) collective-permute-start(f32[4,136,128]{2,1,0:T(8,128)S(1)} %get-tuple-element.11), channel_id=1, source_target_pairs={{0,4},{4,0},{8,12},{12,8},{16,20},{20,16},{24,28},{28,24},{32,36},... | collective-permute-start | bytes 835592 | tf_op jit(solution)/shard_map/ppermute | solution.py:78
  69.1 13.9 %all-to-all-start.2 = ((bf16[32,24,128]{2,1,0:T(8,128)(2,1)}), bf16[32,24,128]{2,1,0:T(8,128)(2,1)S(1)}, u32[]{:S(2)}, u32[]{:S(2)}) async-start(bf16[32,24,128]{2,1,0:T(8,128)(2,1)} %shard_map.70), calls=%async_computation.2 | async-start | bytes 393216 | tf_op jit(solution)/shard_map/all_to_all | solution.py:82
  97.8 3.8 %collective-permute-start.3 = (bf16[32,16,128]{2,1,0:T(8,128)(2,1)S(1)}, bf16[32,16,128]{2,1,0:T(8,128)(2,1)S(1)}, u32[]{:S(2)}, u32[]{:S(2)}) collective-permute-start(bf16[32,16,128]{2,1,0:T(8,128)(2,1)S(1)} %all_to_all.22.near_ref), channel_id=1, source_target_pairs={{0,4},{4,0},{8,12},{12,8},{16,20},{20,16},{24,28},{28,24},{32,36},... | collective-permute-start | bytes 393224 | tf_op jit(solution)/shard_map/ppermute | solution.py:78
